TPU v7x, 32 devices: a whole 2x2x4 slice. The times are simulated.
32 devices in a mesh: tm: 4 (over y, x), space: 2 (over core), dp: 4 (over z).
Axes of the slice: x: 2, y: 2, z: 4, core: 2. Of those that a mesh axis runs over, the one named last changes fastest.
Arguments:
- projected: bfloat16 [16, 1024, 3, 40, 128], P(('dp', 'tm'), None, None, 'space'), parts along dimension 0, may hold values from -256 to 256
- q_gain: float32 [40, 128], P('space'), may hold values from 0.1 to 1.9
- k_gain: float32 [40, 128], P('space'), may hold values from 0.1 to 1.9
- head_weight: float32 [40, 128], P('space'), may hold values from -0.078125 to 0.078125
- step_scale: float32 [4, 40, 128], P(None, 'space'), may hold values from 0.5 to 1.5
- timestep: int32 [16], P('dp'), parts along dimension 0, may hold values from 0 to 3
- frame_count: int32 [4096], P('dp'), parts along dimension 0, may hold values from 1 to 4
Outputs:
- logits: float32 [16, 1024], P(('dp', 'tm'), 'space'), parts along dimension 0
There are 4 independent parts, one for each index of `dp`. A program takes and returns all parts, laid end to end along the dimension named above; an argument that names none is the same for every part. Nothing has to cross between parts.
All inputs are finite; a program needn't handle non-finite values.
Results may differ from a plain program's by a relative error of at most 0.01.
Values may be sent and summed in bfloat16 or wider, within the bound.
No kernel may reach another device: no remote copies, remote signals or barrier semaphores. Data moves between devices by JAX's collectives and lax.ppermute only.
A program may use at most 128 MiB of HBM per device.

v0:
```python
import jax
import jax.numpy as jnp
from jax import lax
from jax.sharding import PartitionSpec as P

HEADS = 40
HEAD = 128


epsilon = 1e-06


def on_device(projected, q_gain, k_gain, head_weight, step_scale, timestep, frame_count):
    channels = HEADS * HEAD
    scaling = HEAD ** (-0.5)
    shard_rows = projected[0]
    queries = shard_rows[:, 0]
    key_rows = shard_rows[:, 1]
    values = shard_rows[:, 2]
    query_sums = jnp.sum(jnp.square(queries.astype(jnp.float32)), axis=(1, 2))
    key_sums = jnp.sum(jnp.square(key_rows.astype(jnp.float32)), axis=(1, 2))
    query_total, key_total = lax.psum((query_sums, key_sums), "space")

    def normalize(features_in, sum_squares, gain_row):
        factor = lax.rsqrt(sum_squares / channels + epsilon)
        scaled = (features_in.astype(jnp.float32) * factor[:, None, None] * gain_row).astype(
            jnp.bfloat16
        )
        return jnp.transpose(scaled, (1, 0, 2))

    q_heads = normalize(queries, query_total, q_gain)
    k_heads = normalize(key_rows, key_total, k_gain)

    def one_head(head_index):
        query_head = lax.dynamic_index_in_dim(q_heads, head_index, 0, keepdims=False)
        key_head = lax.dynamic_index_in_dim(k_heads, head_index, 0, keepdims=False)
        value_head = lax.dynamic_index_in_dim(values, head_index, 1, keepdims=False)
        scores = (
            lax.dot_general(
                query_head, key_head, (((1,), (1,)), ((), ())), preferred_element_type=jnp.float32
            )
            * scaling
        )
        row_max = jnp.max(scores, axis=1, keepdims=True)
        exponent = jnp.exp(scores - row_max)
        weights = (exponent / jnp.sum(exponent, axis=1, keepdims=True)).astype(jnp.bfloat16)
        return jnp.dot(weights, value_head, preferred_element_type=jnp.float32).astype(jnp.bfloat16)

    spatial_out = lax.optimization_barrier(lax.map(one_head, jnp.arange(q_heads.shape[0])))
    query_far = lax.all_to_all(q_heads[:, None], "tm", split_axis=2, concat_axis=1, tiled=True)
    key_far = lax.all_to_all(k_heads[:, None], "tm", split_axis=2, concat_axis=1, tiled=True)
    spatial_far = lax.all_to_all(
        spatial_out[:, None], "tm", split_axis=2, concat_axis=1, tiled=True
    )
    block = query_far.shape[2]
    block_counts = lax.dynamic_slice_in_dim(frame_count, lax.axis_index("tm") * block, block)
    scores = (
        jnp.einsum("hfpe,hgpe->hpfg", query_far, key_far, preferred_element_type=jnp.float32)
        * scaling
    )
    live_frames = jnp.arange(query_far.shape[1], dtype=jnp.int32)[None, :] < block_counts[:, None]
    scores = jnp.where(live_frames[None, :, None, :], scores, -1e30)
    row_max = jnp.max(scores, axis=3, keepdims=True)
    exponent = jnp.exp(scores - row_max)
    weights = (exponent / jnp.sum(exponent, axis=3, keepdims=True)).astype(jnp.bfloat16)
    temporal_mix = jnp.einsum(
        "hpfg,hgpe->hfpe", weights, spatial_far, preferred_element_type=jnp.float32
    ).astype(jnp.bfloat16)
    temporal_mix, spatial_far = (lax.optimization_barrier(temporal_mix), spatial_far)
    own_step = lax.dynamic_index_in_dim(timestep, lax.axis_index("tm"), 0, keepdims=False)
    row_scale = lax.dynamic_index_in_dim(step_scale, own_step, 0, keepdims=False)
    mixed_home = lax.all_to_all(temporal_mix, "tm", split_axis=1, concat_axis=2, tiled=True)
    combined = spatial_out.astype(jnp.float32) + mixed_home[:, 0].astype(jnp.float32)
    modulated = combined * row_scale[:, None, :]
    dot_home = jnp.sum(modulated * head_weight[:, None, :], axis=(0, 2))
    square_home = jnp.sum(modulated * modulated, axis=(0, 2))
    dot_mine, square_mine = (
        lax.psum_scatter(dot_home, "space", scatter_dimension=0, tiled=True),
        lax.psum_scatter(square_home, "space", scatter_dimension=0, tiled=True),
    )
    logits = dot_mine * lax.rsqrt(square_mine / channels + epsilon)
    return logits[None, :]


def solution(mesh):
    in_specs = (
        P(("dp", "tm"), None, None, "space", None),
        P("space", None),
        P("space", None),
        P("space", None),
        P(None, "space", None),
        P("dp"),
        P("dp"),
    )
    out_specs = P(("dp", "tm"), "space")
    return jax.shard_map(
        on_device, mesh=mesh, in_specs=in_specs, out_specs=out_specs, check_vma=False
    )
```

profile of v0, /device:TPU:1, one launch (start us, length us, event | category | flops | bytes accessed | tf_op | source)
XLA Modules:
  0.0 477.5 jit_solution(18444918203010089414)
XLA Ops:
  0.0 31.2 %copy.69 = bf16[1,1024,3,20,128]{4,3,1,2,0:T(8,128)(2,1)S(1)} copy(bf16[1,1024,3,20,128]{4,1,3,2,0:T(8,128)(2,1)} %param.9) | data formatting | bytes 31457280 | tf_op args[0]
  31.2 6.5 %copy-done.1 = bf16[1,1024,3,20,128]{4,3,1,2,0:T(8,128)(2,1)} copy-done((bf16[1,1024,3,20,128]{4,3,1,2,0:T(8,128)(2,1)}, bf16[1,1024,3,20,128]{4,3,1,2,0:T(8,128)(2,1)S(1)}, u32[]{:S(2)}) %copy-start.1) | copy-done | bytes 15728664
  37.7 13.3 %fusion.19 = (f32[1024]{0:T(1024)S(1)}, f32[1024]{0:T(1024)S(1)}) fusion(bf16[1024,3,20,128]{3,2,0,1:T(8,128)(2,1)S(1)} %bitcast.86), kind=kLoop, calls=%fused_computation.27 | loop fusion | flops 15726592 | bytes 10493952 | tf_op jit(solution)/shard_map/reduce_sum | solution.py:21
  51.0 2.5 all-reduce.3
  53.5 14.1 %fusion.34 = (bf16[20,1,1024,128]{3,0,1,2:T(8,128)(2,1)}, bf16[20,1024,128]{2,0,1:T(8,128)(2,1)}, bf16[20,1024,128]{2,0,1:T(8,128)(2,1)}, bf16[20,1,1024,128]{3,0,1,2:T(8,128)(2,1)}) fusion(f32[20,128]{1,0:T(8,128)S(1)} %copy-done.3, f32[1024]{0:T(1024)S(1)} %get-tuple-element.87, bf16[1024,3,20,128]{3,2,0,1:T(8,128)(2,1)} %bitcast.87, ...), kind=kLoop, calls=%fused_computation.48 | loop fusion | flops 20971520 | bytes 31485952 | tf_op jit(solution)/shard_map/broadcast_in_dim | solution.py:50
  67.6 5.4 %all-to-all-start.1 = ((bf16[20,1,1024,128]{3,0,1,2:T(8,128)(2,1)}), bf16[20,1,1024,128]{3,0,1,2:T(8,128)(2,1)}, u32[]{:S(2)}, u32[]{:S(2)}) async-start(bf16[20,1,1024,128]{3,0,1,2:T(8,128)(2,1)} %get-tuple-element.78), calls=%async_computation.1 | async-start | bytes 12582912 | tf_op jit(solution)/shard_map/all_to_all | solution.py:50
  73.0 6.4 %copy.35 = bf16[20,1024,128]{2,1,0:T(8,128)(2,1)} copy(bf16[20,1024,128]{2,0,1:T(8,128)(2,1)} %get-tuple-element.79) | data formatting | bytes 10485760 | tf_op jit(solution)/shard_map/while | solution.py:49
  79.5 3.4 copy.36
  82.9 3.9 slice_bitcast_fusion
  86.7 3.5 copy.37
  90.2 53.7 %all-to-all-done.1 = bf16[20,1,1024,128]{3,0,1,2:T(8,128)(2,1)} async-done(((bf16[20,1,1024,128]{3,0,1,2:T(8,128)(2,1)}), bf16[20,1,1024,128]{3,0,1,2:T(8,128)(2,1)}, u32[]{:S(2)}, u32[]{:S(2)}) %all-to-all-start.1) | async-done | bytes 5242912 | tf_op jit(solution)/shard_map/all_to_all | solution.py:50
  143.9 5.2 %all-to-all-start.2 = ((bf16[20,1,1024,128]{3,0,1,2:T(8,128)(2,1)}), bf16[20,1,1024,128]{3,0,1,2:T(8,128)(2,1)}, u32[]{:S(2)}, u32[]{:S(2)}) async-start(bf16[20,1,1024,128]{3,0,1,2:T(8,128)(2,1)} %get-tuple-element.83), calls=%async_computation.2 | async-start | bytes 12582912 | tf_op jit(solution)/shard_map/all_to_all | solution.py:51
  149.2 150.7 %while.10 = (s32[]{:T(128)}, bf16[20,1024,128]{2,1,0:T(8,128)(2,1)}, s32[20]{0:T(128)S(1)}, bf16[20,1024,128]{2,1,0:T(8,128)(2,1)}, bf16[20,1024,128]{2,1,0:T(8,...) while((s32[]{:T(128)}, bf16[20,1024,128]{2,1,0:T(8,128)(2,1)}, ...), condition=%wide.region_7.8_spmd, body=%wide.region_4.7_spmd.sunk | while | flops 546437120 | bytes 13653647 | solution.py:49
  153.9 2.8 fusion.52
  159.0 1.7 multiply_reduce_fusion.4
  161.5 2.8 fusion.52
  169.0 2.8 fusion.52
  176.6 2.8 fusion.52
  184.1 2.8 fusion.52
  191.6 2.8 fusion.52
  199.2 2.8 fusion.52
  204.2 1.7 multiply_reduce_fusion.4
  206.7 2.8 fusion.52
  214.3 2.8 fusion.52
  221.8 2.8 fusion.52
  229.3 2.8 fusion.52
  236.8 2.8 fusion.52
  244.3 2.8 fusion.52
  251.9 2.8 fusion.52
  259.4 2.8 fusion.52
  266.9 2.8 fusion.52
  274.5 2.8 fusion.52
  282.0 2.8 fusion.52
  289.6 2.8 fusion.52
  297.1 2.8 fusion.52
  299.9 8.7 %copy.70 = bf16[20,1024,128]{2,0,1:T(8,128)(2,1)} copy(bf16[20,1024,128]{2,1,0:T(8,128)(2,1)} %get-tuple-element.37) | data formatting | bytes 10485760 | tf_op jit(solution)/shard_map/optimization_barrier | solution.py:49
  308.6 5.5 %all-to-all-start = ((bf16[20,1,1024,128]{3,0,1,2:T(8,128)(2,1)}), bf16[20,1,1024,128]{3,0,1,2:T(8,128)(2,1)}, u32[]{:S(2)}, u32[]{:S(2)}) async-start(bf16[20,1,1024,128]{3,0,1,2:T(8,128)(2,1)} %bitcast.89), calls=%async_computation | async-start | bytes 12582912 | tf_op jit(solution)/shard_map/all_to_all | solution.py:52
  314.9 24.6 %fusion.23 = f32[20,256,4,4]{2,3,1,0:T(4,128)} fusion(bf16[20,4,256,128]{3,0,2,1:T(8,128)(2,1)} %bitcast.19, bf16[20,4,256,128]{3,0,2,1:T(8,128)(2,1)} %bitcast.16), kind=kOutput, calls=%fused_computation.38 | convolution fusion | flops 20971520 | bytes 10813440 | tf_op jit(solution)/shard_map/hfpe,hgpe->hpfg/dot_general | solution.py:58
  339.5 7.6 %copy.45 = f32[20,256,4,4]{1,3,2,0:T(4,128)S(1)} copy(f32[20,256,4,4]{2,3,1,0:T(4,128)} %fusion.23) | data formatting | bytes 655360 | tf_op jit(solution)/shard_map/hfpe,hgpe->hpfg/dot_general | solution.py:58
  347.7 5.3 %copy.47 = bf16[20,256,4,4]{3,2,1,0:T(4,128)(2,1)} copy(bf16[20,256,4,4]{1,3,2,0:T(4,128)(2,1)S(1)} %divide_convert_fusion.8) | data formatting | bytes 327680 | tf_op jit(solution)/shard_map/convert_element_type | solution.py:65
  352.9 30.6 %all-to-all-done = bf16[20,1,1024,128]{3,0,1,2:T(8,128)(2,1)} async-done(((bf16[20,1,1024,128]{3,0,1,2:T(8,128)(2,1)}), bf16[20,1,1024,128]{3,0,1,2:T(8,128)(2,1)}, u32[]{:S(2)}, u32[]{:S(2)}) %all-to-all-start) | async-done | bytes 5242912 | tf_op jit(solution)/shard_map/all_to_all | solution.py:52
  383.5 13.5 %convert_bitcast_fusion = bf16[20,4,256,128]{3,1,2,0:T(4,128)(2,1)S(1)} fusion(bf16[20,256,4,4]{3,2,1,0:T(4,128)(2,1)} %copy.47, bf16[20,4,256,128]{3,0,2,1:T(8,128)(2,1)} %bitcast.14), kind=kOutput, calls=%fused_computation.43 | convolution fusion | flops 23592960 | bytes 10649600 | tf_op jit(solution)/shard_map/hpfg,hgpe->hfpe/dot_general | solution.py:66
  397.0 3.7 copy.48
  400.7 5.2 %all-to-all-start.3 = ((bf16[20,4,256,128]{3,2,0,1:T(8,128)(2,1)}), bf16[20,4,256,128]{3,2,0,1:T(8,128)(2,1)}, u32[]{:S(2)}, u32[]{:S(2)}) async-start(bf16[20,4,256,128]{3,2,0,1:T(8,128)(2,1)} %copy.48), calls=%async_computation.3 | async-start | bytes 10485760 | tf_op jit(solution)/shard_map/all_to_all | solution.py:72
  409.7 54.2 %all-to-all-done.3 = bf16[20,4,256,128]{3,2,0,1:T(8,128)(2,1)} async-done(((bf16[20,4,256,128]{3,2,0,1:T(8,128)(2,1)}), bf16[20,4,256,128]{3,2,0,1:T(8,128)(2,1)}, u32[]{:S(2)}, u32[]{:S(2)}) %all-to-all-start.3) | async-done | bytes 5242912 | tf_op jit(solution)/shard_map/all_to_all | solution.py:72
  463.9 3.1 copy.49
  467.0 5.7 %multiply_reduce_fusion.2 = (f32[1024]{0:T(1024)S(1)}, f32[1024]{0:T(1024)S(1)}) fusion(bf16[20,1024,128]{2,1,0:T(8,128)(2,1)} %get-tuple-element.37, bf16[20,4,256,128]{3,2,1,0:T(8,128)(2,1)S(1)} %copy.49, f32[20,128]{1,0:T(8,128)S(1)} %copy-done.5, f32[20,128]{1,0:T(8,128)S(1)} %bitcast.90), kind=kLoop, calls=%fused_computation.33 | loop fusion | flops 20969472 | bytes 10514432 | tf_op jit(solution)/shard_map/reduce_sum | solution.py:75
  472.7 3.7 all-reduce.2
  (86 shorter events, 60.9 us)
Async XLA Ops:
  0.0 408.4 %copy-start = (f32[4,20,128]{2,0,1:T(4,128)S(1)}, f32[4,20,128]{2,0,1:T(4,128)}, u32[]{:S(2)}) copy-start(f32[4,20,128]{2,0,1:T(4,128)} %param.13) | copy-start | bytes 122884
  31.2 6.5 %copy-start.1 = (bf16[1,1024,3,20,128]{4,3,1,2,0:T(8,128)(2,1)}, bf16[1,1024,3,20,128]{4,3,1,2,0:T(8,128)(2,1)S(1)}, u32[]{:S(2)}) copy-start(bf16[1,1024,3,20,128]{4,3,1,2,0:T(8,128)(2,1)S(1)} %copy.69) | copy-start | bytes 47185924
  37.6 15.8 %copy-start.3 = (f32[20,128]{1,0:T(8,128)S(1)}, f32[20,128]{1,0:T(8,128)}, u32[]{:S(2)}) copy-start(f32[20,128]{1,0:T(8,128)} %param.10) | copy-start | bytes 30724
  37.6 15.8 %copy-start.4 = (f32[20,128]{1,0:T(8,128)S(1)}, f32[20,128]{1,0:T(8,128)}, u32[]{:S(2)}) copy-start(f32[20,128]{1,0:T(8,128)} %param.11) | copy-start | bytes 30724
  67.6 76.4 %all-to-all-start.1 = ((bf16[20,1,1024,128]{3,0,1,2:T(8,128)(2,1)}), bf16[20,1,1024,128]{3,0,1,2:T(8,128)(2,1)}, u32[]{:S(2)}, u32[]{:S(2)}) async-start(bf16[20,1,1024,128]{3,0,1,2:T(8,128)(2,1)} %get-tuple-element.78), calls=%async_computation.1 | async-start | bytes 12582912 | tf_op jit(solution)/shard_map/all_to_all | solution.py:50
  73.0 6.4 %copy-start.2 = (bf16[20,1024,128]{2,0,1:T(8,128)(2,1)S(1)}, bf16[20,1024,128]{2,0,1:T(8,128)(2,1)}, u32[]{:S(2)}) copy-start(bf16[20,1024,128]{2,0,1:T(8,128)(2,1)} %get-tuple-element.82) | copy-start | bytes 15728644
  143.9 164.7 %all-to-all-start.2 = ((bf16[20,1,1024,128]{3,0,1,2:T(8,128)(2,1)}), bf16[20,1,1024,128]{3,0,1,2:T(8,128)(2,1)}, u32[]{:S(2)}, u32[]{:S(2)}) async-start(bf16[20,1,1024,128]{3,0,1,2:T(8,128)(2,1)} %get-tuple-element.83), calls=%async_computation.2 | async-start | bytes 12582912 | tf_op jit(solution)/shard_map/all_to_all | solution.py:51
  308.6 74.9 %all-to-all-start = ((bf16[20,1,1024,128]{3,0,1,2:T(8,128)(2,1)}), bf16[20,1,1024,128]{3,0,1,2:T(8,128)(2,1)}, u32[]{:S(2)}, u32[]{:S(2)}) async-start(bf16[20,1,1024,128]{3,0,1,2:T(8,128)(2,1)} %bitcast.89), calls=%async_computation | async-start | bytes 12582912 | tf_op jit(solution)/shard_map/all_to_all | solution.py:52
  400.7 5.2 %copy-start.6 = (s32[4]{0:T(128)S(1)}, s32[4]{0:T(128)}, u32[]{:S(2)}) copy-start(s32[4]{0:T(128)} %param.14) | copy-start | bytes 52
  400.7 7.8 %copy-start.7 = (u32[32]{0:T(128)S(1)}, u32[32]{0:T(128)}, u32[]{:S(2)}) copy-start(u32[32]{0:T(128)} %constant.66) | copy-start | bytes 388
  400.7 63.3 %all-to-all-start.3 = ((bf16[20,4,256,128]{3,2,0,1:T(8,128)(2,1)}), bf16[20,4,256,128]{3,2,0,1:T(8,128)(2,1)}, u32[]{:S(2)}, u32[]{:S(2)}) async-start(bf16[20,4,256,128]{3,2,0,1:T(8,128)(2,1)} %copy.48), calls=%async_computation.3 | async-start | bytes 10485760 | tf_op jit(solution)/shard_map/all_to_all | solution.py:72
  409.7 57.3 %copy-start.5 = (f32[20,128]{1,0:T(8,128)S(1)}, f32[20,128]{1,0:T(8,128)}, u32[]{:S(2)}) copy-start(f32[20,128]{1,0:T(8,128)} %param.12) | copy-start | bytes 30724
where the time goes:
time: 486 us; the launch traced here: 478 us
  waiting for transfers between devices  138 us (28%)
  matrix products  129 us (27%)
  local copies, waits for them, and re-layouts  96.7 us (20%)
  other arithmetic  49 us (10%)
  loops' own time  33.9 us (7%)
  starting transfers between devices  21.3 us (4%)
  blocking collectives  6.17 us (1%)
    dot_general x20, matrix products, one_head(): jnp.dot(weights, value_head, preferred_element_type=jnp.float32)  55.7 us
    all_to_all x1, waiting for transfers between devices, on_device(): lax.all_to_all(temporal_mix, 'tm', split_axis=1, concat_axis=2, tiled=True)  54.2 us
    all_to_all x1, waiting for transfers between devices, on_device(): lax.all_to_all(q_heads[:, None], 'tm', split_axis=2, concat_axis=1, tiled...  53.7 us
    unnamed x19, local copies, waits for them, and re-layouts  38.2 us
    dot_general x20, matrix products, one_head(): lax.dot_general(query_head, key_head, (((1,), (1,)), ((), ())), preferred...  34.9 us
    another operation x1, loops' own time, on_device(): lax.map(one_head, jnp.arange(q_heads.shape[0]))  33.9 us
    all_to_all x1, waiting for transfers between devices, on_device(): lax.all_to_all(spatial_out[:, None], 'tm', split_axis=2, concat_axis=1, t...  30.6 us
    dot_general x1, matrix products, on_device(): jnp.einsum('hfpe,hgpe->hpfg', query_far, key_far, preferred_element_type=...  24.6 us
  transfers between devices with their start and end apart: 4, of which 3 were waited for; matrix products, arithmetic and copies ran while one was open for 38% of the time, Pallas kernels for 0%

commit v1 on v0

v1 whole, which is shorter than its diff:
```python
import functools

import jax
import jax.numpy as jnp
from jax import lax
from jax.experimental import pallas as pl
from jax.experimental.pallas import tpu as pltpu
from jax.sharding import PartitionSpec as P

HEADS = 40
HEAD = 128
CHANNELS = HEADS * HEAD
EPSILON = 1e-06
LOG2E = 1.4426950408889634
SCALE2 = HEAD ** (-0.5) * LOG2E
MASKED = -1e30
NT = (((1,), (1,)), ((), ()))
VMEM_LIMIT = 48 * 1024 * 1024


def lane_sums(acc):
    pieces = []
    for start in range(0, acc.shape[0], HEAD):
        pieces.append(jnp.sum(acc[start : start + HEAD].T, axis=0, keepdims=True))
    return jnp.concatenate(pieces, axis=1)


def spread_rows(row):
    pieces = []
    for start in range(0, row.shape[1], HEAD):
        piece = jnp.broadcast_to(row[:, start : start + HEAD], (HEAD, HEAD))
        pieces.append(piece.T)
    return jnp.concatenate(pieces, axis=0)


def store_shares(count_ref, rank_ref, frames_ref=None):
    shares, width = rank_ref.shape
    lines = width // HEAD
    many = jnp.where(count_ref[...] >= 2, 1.0, 0.0)
    row = lax.broadcasted_iota(jnp.int32, (HEAD, HEAD), 0)
    column = lax.broadcasted_iota(jnp.int32, (HEAD, HEAD), 1)
    upto = jnp.dot(
        many, jnp.where(row <= column, 1.0, 0.0), preferred_element_type=jnp.float32
    )
    lane = lax.broadcasted_iota(jnp.int32, (1, HEAD), 1).astype(jnp.float32)
    for share in range(shares):
        total = jnp.zeros((1, 1), jnp.float32)
        before = []
        for line in range(share * lines, (share + 1) * lines):
            before.append(upto[line : line + 1] - many[line : line + 1] + total)
            total = total + upto[line : line + 1, HEAD - 1 :]
        for i in range(lines):
            line = share * lines + i
            later = total + (lane + float(i * HEAD)) - before[i]
            rank = jnp.where(many[line : line + 1] > 0.5, before[i], later)
            here = (slice(share, share + 1), slice(i * HEAD, (i + 1) * HEAD))
            rank_ref[here] = rank.astype(jnp.int32)
            if frames_ref is not None:
                frames_ref[here] = count_ref[line : line + 1].astype(jnp.float32)


def picks(rank_ref, owner, each, first, size):
    width = rank_ref.shape[1]
    place = lax.broadcasted_iota(jnp.int32, (size, width), 0) + first
    return rank_ref[pl.ds(lax.div(owner, each), 1), :] == place * each + lax.rem(owner, each)


def gather_kernel(slots_ref, count_ref, *refs, offsets, each, first, with_sums):
    number = len(offsets)
    sources = 2 if with_sums else 2 * number
    sources, refs = refs[:sources], refs[sources:]
    outs, refs = refs[:number], refs[number:]
    if with_sums:
        out_ref, rank_ref, pick_ref, acc_ref = refs
    else:
        rank_ref, pick_ref = refs
    step = pl.program_id(0)
    size = outs[0].shape[2]

    @pl.when(step == 0)
    def _():
        store_shares(count_ref, rank_ref)
        for i, offset in enumerate(offsets):
            hit = picks(rank_ref, slots_ref[offset], each, first, size)
            pick_ref[i] = jnp.where(hit, 1.0, 0.0).astype(jnp.bfloat16)
        if with_sums:
            acc_ref[...] = jnp.zeros_like(acc_ref)

    width = rank_ref.shape[1]
    for i, offset in enumerate(offsets):
        start = pl.multiple_of(lax.div(slots_ref[offset], each) * width, width)
        for h in range(outs[i].shape[1]):
            if with_sums:
                rows = [source[0, h, pl.ds(start, width), :] for source in sources]
            else:
                rows = [source[0, h] for source in sources[2 * i : 2 * i + 2]]
            rows = jnp.concatenate(rows, axis=1)
            rows = jnp.dot(pick_ref[i], rows, preferred_element_type=jnp.float32)
            rows = rows.astype(jnp.bfloat16)
            outs[i][0, h] = rows[:, :HEAD]
            outs[i][1, h] = rows[:, HEAD:]
    if with_sums:
        for which in range(2):
            sums = acc_ref[which]
            for h in range(sources[which].shape[1]):
                wide = sources[which][0, h].astype(jnp.float32)
                sums = sums + wide * wide
            acc_ref[which] = sums

        @pl.when(step == pl.num_programs(0) - 1)
        def _():
            for which in range(2):
                out_ref[which : which + 1] = lane_sums(acc_ref[which])


def gather(slots, counts, x, offsets, each, shares, first, size, at, heads, with_sums=False):
    pixels = x.shape[2]
    step = max(i for i in range(1, 6) if heads % i == 0 and at % i == 0)
    step = step // 2 if step == heads and step % 2 == 0 else step
    skip = at // step
    width = pixels // shares

    def source(which, offset):
        return pl.BlockSpec(
            (1, step, width, HEAD), lambda h, s: (which, skip + h, lax.div(s[offset], each), 0)
        )

    in_specs = [pl.BlockSpec(counts.shape, lambda h, s: (0, 0))]
    if not with_sums:
        in_specs += [source(which, offset) for offset in offsets for which in range(2)]
    out_specs = [pl.BlockSpec((2, step, size, HEAD), lambda h, s: (0, h, 0, 0))] * len(offsets)
    out_shape = [jax.ShapeDtypeStruct((2, heads, size, HEAD), jnp.bfloat16)] * len(offsets)
    scratch = [
        pltpu.VMEM((shares, width), jnp.int32),
        pltpu.VMEM((len(offsets), size, width), jnp.bfloat16),
    ]
    if with_sums:
        for which in range(2):
            in_specs.append(
                pl.BlockSpec(
                    (1, step, pixels, HEAD), lambda h, s, which=which: (which, skip + h, 0, 0)
                )
            )
        out_specs.append(pl.BlockSpec((2, pixels), lambda h, s: (0, 0)))
        out_shape.append(jax.ShapeDtypeStruct((2, pixels), jnp.float32))
        scratch.append(pltpu.VMEM((2, pixels, HEAD), jnp.float32))
    return pl.pallas_call(
        functools.partial(
            gather_kernel, offsets=tuple(offsets), each=each, first=first, with_sums=with_sums
        ),
        grid_spec=pltpu.PrefetchScalarGridSpec(
            num_scalar_prefetch=1,
            grid=(heads // step,),
            in_specs=in_specs,
            out_specs=out_specs,
            scratch_shapes=scratch,
        ),
        out_shape=out_shape,
        compiler_params=pltpu.CompilerParams(vmem_limit_bytes=VMEM_LIMIT),
        cost_estimate=pl.CostEstimate(
            flops=4 * heads * pixels * HEAD,
            bytes_accessed=4 * heads * (len(offsets) * size + pixels) * HEAD,
            transcendentals=0,
        ),
        name="gather_sums" if with_sums else "gather",
    )(slots, counts, *[x] * (len(in_specs) - 1))


def spatial_kernel(
    slots_ref, count_ref, q_ref, k_ref, v_ref, factor_ref, qg_ref, kg_ref, *rest, count, each
):
    outs, rest = rest[:count], rest[count:]
    fq_ref, fk_ref, qn_ref, kn_ref, ve_ref, rank_ref, pick_ref = rest
    width = rank_ref.shape[1]

    @pl.when(pl.program_id(0) == 0)
    def _():
        fq_ref[...] = spread_rows(factor_ref[0:1])
        fk_ref[...] = spread_rows(factor_ref[1:2])
        ve_ref[:, :, HEAD:] = jnp.ones((ve_ref.shape[0], ve_ref.shape[1], HEAD), jnp.bfloat16)
        store_shares(count_ref, rank_ref)
        for slot in range(count):
            hit = picks(rank_ref, slots_ref[slot], each, 0, pick_ref.shape[1])
            pick_ref[slot] = jnp.where(hit, 1.0, 0.0).astype(jnp.bfloat16)

    many = q_ref.shape[1]
    for h in range(many):
        qn = q_ref[0, h].astype(jnp.float32) * fq_ref[...] * qg_ref[h]
        qn_ref[:, h * HEAD : (h + 1) * HEAD] = qn.astype(jnp.bfloat16)
        kn = k_ref[0, h].astype(jnp.float32) * fk_ref[...] * kg_ref[h]
        kn_ref[h] = kn.astype(jnp.bfloat16)
        ve_ref[h, :, :HEAD] = v_ref[0, h]
    for slot in range(count):
        start = pl.multiple_of(lax.div(slots_ref[slot], each) * width, width)
        picked = jnp.dot(
            pick_ref[slot], qn_ref[pl.ds(start, width), :], preferred_element_type=jnp.float32
        ).astype(jnp.bfloat16)
        for h in range(many):
            qn = picked[:, h * HEAD : (h + 1) * HEAD]
            s = lax.dot_general(qn, kn_ref[h], NT, preferred_element_type=jnp.float32)
            top = jnp.max(s, axis=1, keepdims=True)
            p = jnp.exp2(s * SCALE2 - top * SCALE2).astype(jnp.bfloat16)
            o = jnp.dot(p, ve_ref[h], preferred_element_type=jnp.float32)
            outs[slot][h] = (o[:, :HEAD] / o[:, HEAD:]).astype(jnp.bfloat16)


def spatial(slots, counts, x, factors, q_gain, k_gain, first, size, count, each, shares):
    pixels = x.shape[2]
    block, width = pixels // count, pixels // shares

    def rows(which):
        return pl.BlockSpec((1, step, pixels, HEAD), lambda h, s: (which, skip + h, 0, 0))

    step = 2 if size % 2 == 0 and first % 2 == 0 else 1
    skip = first // step
    gain = pl.BlockSpec((step, 1, HEAD), lambda h, s: (skip + h, 0, 0))
    return pl.pallas_call(
        functools.partial(spatial_kernel, count=count, each=each),
        grid_spec=pltpu.PrefetchScalarGridSpec(
            num_scalar_prefetch=1,
            grid=(size // step,),
            in_specs=[
                pl.BlockSpec(counts.shape, lambda h, s: (0, 0)),
                rows(0),
                rows(1),
                rows(2),
                pl.BlockSpec((2, pixels), lambda h, s: (0, 0)),
                gain,
                gain,
            ],
            out_specs=[pl.BlockSpec((step, block, HEAD), lambda h, s: (h, 0, 0))] * count,
            scratch_shapes=[
                pltpu.VMEM((pixels, HEAD), jnp.float32),
                pltpu.VMEM((pixels, HEAD), jnp.float32),
                pltpu.VMEM((pixels, step * HEAD), jnp.bfloat16),
                pltpu.VMEM((step, pixels, HEAD), jnp.bfloat16),
                pltpu.VMEM((step, pixels, 2 * HEAD), jnp.bfloat16),
                pltpu.VMEM((shares, width), jnp.int32),
                pltpu.VMEM((count, block, width), jnp.bfloat16),
            ],
        ),
        out_shape=[jax.ShapeDtypeStruct((size, block, HEAD), jnp.bfloat16)] * count,
        compiler_params=pltpu.CompilerParams(vmem_limit_bytes=VMEM_LIMIT),
        cost_estimate=pl.CostEstimate(
            flops=8 * size * pixels * pixels * HEAD,
            bytes_accessed=8 * size * pixels * HEAD,
            transcendentals=size * pixels * pixels,
        ),
        name="spatial_attention",
    )(slots, counts, x, x, x, factors, q_gain, k_gain)


def far_sums_kernel(*refs):
    far, (out_ref, acc_ref) = refs[:-2], refs[-2:]
    head = pl.program_id(0)
    block = far[0].shape[2]

    @pl.when(head == 0)
    def _():
        acc_ref[...] = jnp.zeros_like(acc_ref)

    for i, ref in enumerate(far):
        which, at = i % 2, i // 2 * block
        sums = acc_ref[which, at : at + block]
        for h in range(ref.shape[1]):
            wide = ref[0, h].astype(jnp.float32)
            sums = sums + wide * wide
        acc_ref[which, at : at + block] = sums

    @pl.when(head == pl.num_programs(0) - 1)
    def _():
        for which in range(2):
            out_ref[which : which + 1] = lane_sums(acc_ref[which])


def far_sums(far, heads):
    block = far[0][0].shape[2]
    rows = len(far) // 2 * block
    step = max(i for i in range(1, 6) if all(n % i == 0 for n in (heads, *[f[2] for f in far])))
    return pl.pallas_call(
        far_sums_kernel,
        grid=(heads // step,),
        in_specs=[
            pl.BlockSpec(
                (1, step, block, HEAD),
                lambda h, place=place, skip=at // step: (place, skip + h, 0, 0),
            )
            for _, place, at in far
        ],
        out_specs=pl.BlockSpec((2, rows), lambda h: (0, 0)),
        out_shape=jax.ShapeDtypeStruct((2, rows), jnp.float32),
        scratch_shapes=[pltpu.VMEM((2, rows, HEAD), jnp.float32)],
        compiler_params=pltpu.CompilerParams(vmem_limit_bytes=VMEM_LIMIT),
        cost_estimate=pl.CostEstimate(
            flops=4 * heads * rows * HEAD, bytes_accessed=4 * heads * rows * HEAD, transcendentals=0
        ),
        name="far_sums",
    )(*[array for array, _, _ in far])


def weights_kernel(
    slots_ref, count_ref, factor_ref, frame_ref, qg_ref, kg_ref, *rest, each, first, part
):
    far, (out_ref, fq_ref, fk_ref, rank_ref, frames_ref, bias_ref) = rest[:-6], rest[-6:]
    count = len(far) // 2
    size = far[0].shape[2]
    wide = count * part

    @pl.when(pl.program_id(0) == 0)
    def _():
        fq_ref[...] = spread_rows(factor_ref[0:1])
        fk_ref[...] = spread_rows(factor_ref[1:2])
        store_shares(count_ref, rank_ref, frames_ref)
        me = slots_ref[0]
        frames = frames_ref[pl.ds(lax.div(me, each), 1), :]
        hit = picks(rank_ref, me, each, first, size)
        frames = jnp.sum(jnp.where(hit, frames, 0.0), axis=1, keepdims=True)
        row = lax.broadcasted_iota(jnp.int32, (wide, wide), 0)
        column = lax.broadcasted_iota(jnp.int32, (wide, wide), 1)
        same = ((row - column) & (part - 1)) == 0
        for j in range(size // part):
            held = jnp.concatenate([frames[j * part : (j + 1) * part]] * count, axis=0)
            live = jnp.where(frame_ref[...] < held, 0.0, MASKED)
            bias_ref[j] = jnp.where(same, live, MASKED)

    def normal(which, factor, gain, at):
        pieces = []
        for slot in range(count):
            rows = far[2 * slot + which][0, 0, at : at + part].astype(jnp.float32)
            rows = rows * factor[slot * size + at : slot * size + at + part] * gain
            pieces.append(rows.astype(jnp.bfloat16))
        return jnp.concatenate(pieces, axis=0)

    for j in range(size // part):
        qn = normal(0, fq_ref, qg_ref[0], j * part)
        kn = normal(1, fk_ref, kg_ref[0], j * part)
        s = lax.dot_general(qn, kn, NT, preferred_element_type=jnp.float32) * SCALE2 + bias_ref[j]
        e = jnp.exp2(s - jnp.max(s, axis=1, keepdims=True))
        out_ref[0, j] = (e * (1.0 / jnp.sum(e, axis=1, keepdims=True))).astype(jnp.bfloat16)


def position_factors(parts):
    sums = functools.reduce(jnp.add, [far_sums(far, heads) for far, heads in parts])
    factors = lax.rsqrt(lax.psum(sums, "space") / CHANNELS + EPSILON)
    return jnp.pad(factors, ((0, 0), (0, -factors.shape[1] % HEAD)))


def temporal_weights(
    slots, counts, factors, far, q_gain, k_gain, each, shares, first, part, start, heads
):
    count = len(far) // 2
    size = far[0][0].shape[2]
    rows, wide, subs = count * size, count * part, size // part
    width = counts.size // shares
    padded = factors.shape[1]
    frame = jnp.repeat(slots, part)[None, :].astype(jnp.float32)
    gain = pl.BlockSpec((1, 1, HEAD), lambda h, s: (start + h, 0, 0))
    return pl.pallas_call(
        functools.partial(weights_kernel, each=each, first=first, part=part),
        grid_spec=pltpu.PrefetchScalarGridSpec(
            num_scalar_prefetch=1,
            grid=(heads,),
            in_specs=[
                pl.BlockSpec(counts.shape, lambda h, s: (0, 0)),
                pl.BlockSpec((2, padded), lambda h, s: (0, 0)),
                pl.BlockSpec((1, wide), lambda h, s: (0, 0)),
                gain,
                gain,
            ]
            + [
                pl.BlockSpec(
                    (1, 1, size, HEAD), lambda h, s, place=place, at=at: (place, at + h, 0, 0)
                )
                for _, place, at in far
            ],
            out_specs=pl.BlockSpec((1, subs, wide, wide), lambda h, s: (h, 0, 0, 0)),
            scratch_shapes=[
                pltpu.VMEM((padded, HEAD), jnp.float32),
                pltpu.VMEM((padded, HEAD), jnp.float32),
                pltpu.VMEM((shares, width), jnp.int32),
                pltpu.VMEM((shares, width), jnp.float32),
                pltpu.VMEM((subs, wide, wide), jnp.float32),
            ],
        ),
        out_shape=jax.ShapeDtypeStruct((heads, subs, wide, wide), jnp.bfloat16),
        compiler_params=pltpu.CompilerParams(vmem_limit_bytes=VMEM_LIMIT),
        cost_estimate=pl.CostEstimate(
            flops=2 * heads * rows * wide * HEAD,
            bytes_accessed=4 * heads * rows * HEAD + 2 * heads * rows * wide,
            transcendentals=heads * rows * wide,
        ),
        name="temporal_weights",
    )(slots, counts, factors, frame, q_gain, k_gain, *[array for array, _, _ in far])


def mix_kernel(slots_ref, count_ref, scale_ref, weight_ref, *rest, count, each, part, more):
    mixed, rest = rest[:count], rest[count:]
    weights, rest = rest[: -(count + 3 + more * count)], rest[-(count + 3 + more * count) :]
    before, rest = rest[: more * count], rest[more * count :]
    outs, (dot_ref, square_ref, rank_ref) = rest[:count], rest[count:]
    head = pl.program_id(0)
    block = mixed[0].shape[1]

    @pl.when(head == 0)
    def _():
        dot_ref[...] = jnp.zeros_like(dot_ref)
        square_ref[...] = jnp.zeros_like(square_ref)
        store_shares(count_ref, rank_ref)

    subs = [(ref, j) for ref in weights for j in range(ref.shape[1])]
    for sub, (p_ref, j) in enumerate(subs):
        at = sub * part
        dots = [dot_ref[slot, at : at + part] for slot in range(count)]
        squares = [square_ref[slot, at : at + part] for slot in range(count)]
        for h in range(p_ref.shape[0]):
            o = jnp.concatenate([mixed[slot][h, at : at + part] for slot in range(count)], axis=0)
            t = jnp.dot(p_ref[h, j], o, preferred_element_type=jnp.float32).astype(jnp.bfloat16)
            both = o.astype(jnp.float32) + t.astype(jnp.float32)
            for slot in range(count):
                m = both[slot * part : (slot + 1) * part] * scale_ref[h, slot : slot + 1]
                dots[slot] = dots[slot] + m * weight_ref[h]
                squares[slot] = squares[slot] + m * m
        for slot in range(count):
            dot_ref[slot, at : at + part] = dots[slot]
            square_ref[slot, at : at + part] = squares[slot]

    @pl.when(head == pl.num_programs(0) - 1)
    def _():
        hit = picks(rank_ref, slots_ref[0], each, 0, block)
        for i, out in enumerate(outs):
            for which, ref in enumerate((dot_ref, square_ref)):
                sums = jnp.sum(ref[slots_ref[count + i]], axis=1, keepdims=True)
                sums = jnp.sum(jnp.where(hit, sums, 0.0), axis=0, keepdims=True)
                if more:
                    sums = before[i][which : which + 1] + sums
                out[which : which + 1] = sums


def mix(slots, counts, weights, scales, weight, before, mixed, first, each, shares, part):
    count = len(mixed)
    size, block, _ = mixed[0].shape
    wide = count * part
    rows = count * block
    width = counts.size // shares
    step = max(i for i in range(1, 6) if size % i == 0 and first % i == 0)
    skip = first // step
    out = pl.BlockSpec((2, width), lambda h, s: (0, 0))
    return pl.pallas_call(
        functools.partial(mix_kernel, count=count, each=each, part=part, more=len(before) // count),
        grid_spec=pltpu.PrefetchScalarGridSpec(
            num_scalar_prefetch=1,
            grid=(size // step,),
            in_specs=[
                pl.BlockSpec(counts.shape, lambda h, s: (0, 0)),
                pl.BlockSpec((step, count, HEAD), lambda h, s: (skip + h, 0, 0)),
                pl.BlockSpec((step, 1, HEAD), lambda h, s: (skip + h, 0, 0)),
            ]
            + [pl.BlockSpec((step, block, HEAD), lambda h, s: (h, 0, 0))] * count
            + [
                pl.BlockSpec(
                    (step, *p.shape[1:]),
                    lambda h, s, skip=(first - at) // step: (skip + h, 0, 0, 0),
                )
                for p, at in weights
            ]
            + [out] * len(before),
            out_specs=[out] * count,
            scratch_shapes=[
                pltpu.VMEM((count, block, HEAD), jnp.float32),
                pltpu.VMEM((count, block, HEAD), jnp.float32),
                pltpu.VMEM((shares, width), jnp.int32),
            ],
        ),
        out_shape=[jax.ShapeDtypeStruct((2, width), jnp.float32)] * count,
        compiler_params=pltpu.CompilerParams(vmem_limit_bytes=VMEM_LIMIT),
        cost_estimate=pl.CostEstimate(
            flops=2 * size * rows * wide * HEAD,
            bytes_accessed=2 * size * rows * (HEAD + wide),
            transcendentals=0,
        ),
        name="temporal_mix",
    )(slots, counts, scales, weight, *mixed, *[p for p, _ in weights], *before)


def on_device(
    projected, q_gain, k_gain, head_weight, step_scale, timestep, frame_count, *, count, shares
):
    x = jnp.transpose(projected[0], (1, 2, 0, 3))
    heads, pixels = x.shape[1], x.shape[2]
    block, width, each = pixels // count, pixels // shares, count // shares
    part = 16
    sure = min(block, -(-13 * block // (16 * part)) * part)
    me = lax.axis_index("tm")
    slots = me ^ jnp.arange(count, dtype=jnp.int32)
    counts = frame_count.reshape(pixels // HEAD, HEAD)
    gains = (q_gain[:, None, :], k_gain[:, None, :])

    def swap(value, offset):
        return lax.ppermute(value, "tm", [(i, i ^ offset) for i in range(count)])

    first = heads * 4 // 5 if heads % 20 == 0 else heads
    ranges = [(at, size) for at, size in ((0, first), (first, heads - first)) if size]
    diagonal = {}
    after = slots
    for at, size in reversed(ranges):
        (piece,) = gather(after, counts, x, [count - 1], each, shares, 0, sure, at, size)
        diagonal[at] = swap(piece, count - 1)
        after = lax.optimization_barrier((slots, piece))[0]
    near = range(1, count - 1)
    *pieces, own, sums = gather(
        after, counts, x, [*near, 0], each, shares, 0, sure, 0, heads, True
    )
    sent = [swap(piece, i + 1) for i, piece in enumerate(pieces)]
    totals = lax.psum(sums, "space")
    factors = lax.rsqrt(totals / CHANNELS + EPSILON)

    groups = []
    for at, size in ranges:
        outs = spatial(slots, counts, x, factors, *gains, at, size, count, each, shares)
        groups.append((at, list(outs)))
    last = groups[-1][1][0]

    crowd = jnp.sum((frame_count.reshape(shares, width) >= 2).astype(jnp.float32), axis=1)
    crowd = jnp.max(crowd)
    early = diagonal[ranges[-1][0]]
    *sent, last = lax.optimization_barrier((*sent, *diagonal.values(), last))
    diagonal = dict(zip(diagonal, sent[len(near) :]))
    ready = sent
    far = {}
    for at, size in ranges:
        far[at] = [(pair, place, at) for pair in (own, *sent[: len(near)]) for place in range(2)]
        far[at] += [(diagonal[at], place, 0) for place in range(2)]
    mine = position_factors([(far[at], size) for at, size in ranges])
    weights = {
        at: [
            (
                temporal_weights(
                    slots, counts, mine, far[at], *gains, each, shares, 0, part, at, size
                ),
                at,
            )
        ]
        for at, size in ranges
    }
    p = weights[0][0][0]
    if sure < block:

        def exchanged():
            spare = gather(
                slots, counts, x, range(count), each, shares, sure, block - sure, 0, heads
            )
            spare = lax.all_to_all(jnp.stack(spare)[slots], "tm", 0, 0)[slots]
            spare = [(spare[slot], place, 0) for slot in range(count) for place in range(2)]
            scale = position_factors([(spare, heads)])
            return temporal_weights(
                slots, counts, scale, spare, *gains, each, shares, sure, part, 0, heads
            )

        def single():
            wide = count * part
            row = lax.broadcasted_iota(jnp.int32, (wide, wide), 0)
            column = lax.broadcasted_iota(jnp.int32, (wide, wide), 1)
            hit = ((row - column) % part == 0) & (column // part == me)
            return jnp.broadcast_to(
                hit.astype(jnp.bfloat16), (heads, (block - sure) // part, wide, wide)
            )

        others = lax.cond(crowd > float(sure * each), exchanged, single)
        for at, _ in ranges:
            weights[at].append((others, 0))

    scales = jnp.transpose(step_scale[timestep[slots]], (1, 0, 2))
    weight = head_weight[:, None, :]
    sends = [(outs, offset) for _, outs in groups for offset in range(1, count)]
    for i, (outs, offset) in enumerate(sends):
        after = (early,) if i < 2 else ready if i < 5 else (p,)
        outs[offset] = lax.optimization_barrier((outs[offset], *after))[0]

    core = lax.axis_index("space")
    rounds = [(r, u) for r in range(each) for u in range(shares)]
    frames = [(core - u) % shares * each + (me - r) % each for r, u in rounds]
    order = jnp.concatenate([slots, me ^ jnp.stack(frames)])
    total = []
    for at, outs in groups:
        mixed = [outs[0]] + [swap(outs[offset], offset) for offset in range(1, count)]
        total = mix(
            order, counts, weights[at], scales, weight, total, mixed, at, each, shares, part
        )
    logits = jnp.zeros((width,), jnp.float32)
    for r in range(each):
        sums = jnp.zeros((2, width), jnp.float32)
        for u in range(shares):
            pairs = [
                (
                    (s * each + (f + r) % each) * shares + (f // each + u) % shares,
                    f * shares + s,
                )
                for f in range(count)
                for s in range(shares)
            ]
            sums = sums + lax.ppermute(total[r * shares + u], ("tm", "space"), pairs)
        logits = logits + sums[0] * lax.rsqrt(sums[1] / CHANNELS + EPSILON)
    return logits[None, :]


def solution(mesh):
    in_specs = (
        P(("dp", "tm"), None, None, "space", None),
        P("space", None),
        P("space", None),
        P("space", None),
        P(None, "space", None),
        P("dp"),
        P("dp"),
    )
    return jax.shard_map(
        functools.partial(on_device, count=mesh.shape["tm"], shares=mesh.shape["space"]),
        mesh=mesh,
        in_specs=in_specs,
        out_specs=P(("dp", "tm"), "space"),
        check_vma=False,
    )
```

time: 486 us -> 168 us (0.35); the launches traced: 478 us -> 166 us
  matrix products: 129 us -> 0 us
  waiting for transfers between devices: 138 us -> 29.9 us
  Pallas kernels: 0 us -> 103 us
  local copies, waits for them, and re-layouts: 96.7 us -> 4.81 us
  other arithmetic: 49 us -> 1.66 us
  loops' own time: 33.9 us -> 0.26 us
    all_to_all x4 -> x0, waiting for transfers between devices: 138 us -> none  [the longest x1 54.2 us: on_device(): lax.all_to_all(temporal_mix, 'tm', split_axis=1, concat_axis=2, tiled=True)]
    dot_general x42 -> x0, matrix products: 129 us -> none  [the longest x20 55.7 us: one_head(): jnp.dot(weights, value_head, preferred_element_type=jnp.float32)]
    pallas_call x0 -> x11, Pallas kernels: none -> 103 us  [the longest x2 48.3 us: spatial(): pl.pallas_call(functools.partial(spatial_kernel, count=count, each=each),...]
    unnamed x19 -> x22, local copies, waits for them, and re-layouts: 38.2 us -> 2.06 us
    another operation x1, loops' own time: 33.9 us -> 0.26 us  [on_device(): others = lax.cond(crowd > float(sure * each), exchanged, single)]
    reduce_sum x22 -> x1, other arithmetic: 33.6 us -> 0.12 us  [on_device(): jnp.sum((frame_count.reshape(shares, width) >= 2).astype(jnp.float32), ax...]
    ppermute x0 -> x14, waiting for transfers between devices: none -> 29.9 us  [the longest x10 27.5 us: swap(): return lax.ppermute(value, 'tm', [(i, i ^ offset) for i in range(count)])]
    all_to_all x4 -> x0, starting transfers between devices: 21.3 us -> none  [the longest x1 5.53 us: on_device(): lax.all_to_all(spatial_out[:, None], 'tm', split_axis=2, concat_axis=1, t...]
  transfers between devices with their start and end apart: 4 -> 14, of which waited for: 3 -> 8; matrix products, arithmetic and copies ran while one was open for 38% -> 2% of each run, Pallas kernels for 0% -> 59%
where the time goes in v1:
time: 168 us; the launch traced here: 166 us
  Pallas kernels  103 us (61%)
  waiting for transfers between devices  29.9 us (18%)
  starting transfers between devices  16.6 us (10%)
  blocking collectives  8.86 us (5%)
  local copies, waits for them, and re-layouts  4.81 us (3%)
    pallas_call x2, Pallas kernels, spatial(): pl.pallas_call(functools.partial(spatial_kernel, count=count, each=each),...  48.3 us
    ppermute x10, waiting for transfers between devices, swap(): return lax.ppermute(value, 'tm', [(i, i ^ offset) for i in range(count)])  27.5 us
    pallas_call x3, Pallas kernels, gather(): pl.pallas_call(functools.partial(gather_kernel, offsets=tuple(offsets), e...  20.5 us
    pallas_call x2, Pallas kernels, temporal_weights(): pl.pallas_call(functools.partial(weights_kernel, each=each, first=first,...  18.8 us
    ppermute x10, starting transfers between devices, swap(): return lax.ppermute(value, 'tm', [(i, i ^ offset) for i in range(count)])  10.1 us
    pallas_call x2, Pallas kernels, mix(): pl.pallas_call(functools.partial(mix_kernel, count=count, each=each, part...  9.71 us
    ppermute x4, starting transfers between devices, on_device(): sums = sums + lax.ppermute(total[r * shares + u], ('tm', 'space'), pairs)  6.5 us
    pallas_call x2, Pallas kernels, far_sums(): pl.pallas_call(far_sums_kernel, grid=(heads // step,), in_specs=[pl.Block...  5.92 us
  transfers between devices with their start and end apart: 14, of which 8 were waited for; matrix products, arithmetic and copies ran while one was open for 2% of the time, Pallas kernels for 59%

profile of v1, /device:TPU:1, one launch (start us, length us, event | category | flops | bytes accessed | tf_op | source)
XLA Modules:
  0.0 166.1 jit_solution(3893301485762942901)
XLA Ops:
  0.0 2.5 %gather.29 = bf16[2,4,208,128]{3,2,1,0:T(8,128)(2,1)S(1)} custom-call(s32[4]{0:T(128)S(1)} %iota_xor_fusion.slots_ref, s32[8,128]{1,0:T(8,128)} %bitcast.46, bf16[3,20,1024,128]{3,2,1,0:T(8,128)(2,1)} %bitcast.33, bf16[3,20,1024,128]{3,2,1,0:T(8,128)(2,1)} %bitcast.34), custom_call_target="tpu_custom_call" | custom-call | flops 2097152 | bytes 2523136 | tf_op jit(solution)/shard_map/gather/pallas_call | solution.py:147
  2.5 3.1 %collective-permute-start.2 = (bf16[2,4,208,128]{3,2,1,0:T(8,128)(2,1)S(1)}, bf16[2,4,208,128]{3,2,1,0:T(8,128)(2,1)S(1)}, u32[]{:S(2)}, u32[]{:S(2)}) collective-permute-start(bf16[2,4,208,128]{3,2,1,0:T(8,128)(2,1)S(1)} %gather.29), channel_id=1, source_target_pairs={{0,24},{8,16},{16,8},{24,0},{1,25},{9,17},{17,9},{25,1},{2,26},{10... | collective-permute-start | bytes 1277960 | tf_op jit(solution)/shard_map/ppermute | solution.py:499
  5.6 5.7 %gather.30 = bf16[2,16,208,128]{3,2,1,0:T(8,128)(2,1)} custom-call(s32[4]{0:T(128)S(1)} %iota_xor_fusion.slots_ref, s32[8,128]{1,0:T(8,128)S(1)} %bitcast.47, bf16[3,20,1024,128]{3,2,1,0:T(8,128)(2,1)} %bitcast.35, bf16[3,20,1024,128]{3,2,1,0:T(8,128)(2,1)} %bitcast.36), custom_call_target="tpu_custom_call" | custom-call | flops 8388608 | bytes 10092544 | tf_op jit(solution)/shard_map/gather/pallas_call | solution.py:147
  11.3 0.0 collective-permute-start.3
  11.3 12.3 %gather_sums.1 = (bf16[2,20,208,128]{3,2,1,0:T(8,128)(2,1)}, bf16[2,20,208,128]{3,2,1,0:T(8,128)(2,1)}, bf16[2,20,208,128]{3,2,1,0:T(8,128)(2,1)}, f32[2,1024]{1,0:T(2,128)S(1)}) custom-call(s32[4]{0:T(128)S(1)} %iota_xor_fusion.slots_ref, s32[8,128]{1,0:T(8,128)S(1)} %bitcast.48, bf16[3,20,1024,128]{3,2,1,0:T(8,128)(2,1)} %bitcast.37, ...), custom_call_target="tpu_custom_call" | custom-call | flops 10485760 | bytes 16875520 | tf_op jit(solution)/shard_map/gather_sums/pallas_call | solution.py:147
  23.6 1.4 collective-permute-start
  25.0 1.2 collective-permute-start.1
  26.2 4.0 %psum.21 = f32[2,1024]{1,0:T(2,128)S(1)} all-reduce(f32[2,1024]{1,0:T(2,128)S(1)} %get-tuple-element.62), channel_id=1, replica_groups=mesh['tm'=4,'space'=2,'dp'=4] {'space'}, use_global_device_ids=true, to_apply=%region_0.0 | all-reduce | flops 2048 | bytes 16384 | tf_op jit(solution)/shard_map/psum | solution.py:514
  30.2 36.6 %spatial_attention.3 = (bf16[16,256,128]{2,1,0:T(8,128)(2,1)S(1)}, bf16[16,256,128]{2,1,0:T(8,128)(2,1)}, bf16[16,256,128]{2,1,0:T(8,128)(2,1)}, bf16[16,256,128]{2,1,0:T(8,128)(2,1)}) custom-call(s32[4]{0:T(128)S(1)} %iota_xor_fusion.slots_ref, s32[8,128]{1,0:T(8,128)S(1)} %bitcast.49, bf16[3,20,1024,128]{3,2,1,0:T(8,128)(2,1)} %bitcast.39, ...), custom_call_target="tpu_custom_call" | custom-call | flops 17179869184 | bytes 16777216 | tf_op jit(solution)/shard_map/spatial_attention/pallas_call | solution.py:217
  66.9 1.0 copy-done.8
  67.9 0.2 collective-permute-start.8
  68.1 11.6 %spatial_attention.2 = (bf16[4,256,128]{2,1,0:T(8,128)(2,1)S(1)}, bf16[4,256,128]{2,1,0:T(8,128)(2,1)}, bf16[4,256,128]{2,1,0:T(8,128)(2,1)}, bf16[4,256,128]{2,1,0:T(8,128)(2,1)}) custom-call(s32[4]{0:T(128)S(1)} %iota_xor_fusion.slots_ref, s32[8,128]{1,0:T(8,128)S(1)} %bitcast.50, bf16[3,20,1024,128]{3,2,1,0:T(8,128)(2,1)} %bitcast.42, ...), custom_call_target="tpu_custom_call" | custom-call | flops 4294967296 | bytes 4194304 | tf_op jit(solution)/shard_map/spatial_attention/pallas_call | solution.py:217
  79.8 0.3 collective-permute-start.7
  80.0 17.4 %collective-permute-done.refs_2_.refs_3_.rest_2_.rest_3_ = bf16[2,20,208,128]{3,2,1,0:T(8,128)(2,1)} collective-permute-done((bf16[2,20,208,128]{3,2,1,0:T(8,128)(2,1)}, bf16[2,20,208,128]{3,2,1,0:T(8,128)(2,1)}, u32[]{:S(2)}, u32[]{:S(2)}) %collective-permute-start) | collective-permute-done | bytes 2129952 | tf_op jit(solution)/shard_map/ppermute | solution.py:499
  97.4 0.8 collective-permute-done.1.refs_4_.refs_5_.rest_4_.rest_5_
  98.1 2.4 %collective-permute-start.9 = (bf16[16,256,128]{2,1,0:T(8,128)(2,1)}, bf16[16,256,128]{2,1,0:T(8,128)(2,1)}, u32[]{:S(2)}, u32[]{:S(2)}) collective-permute-start(bf16[16,256,128]{2,1,0:T(8,128)(2,1)} %get-tuple-element.83), channel_id=1, source_target_pairs={{0,24},{8,16},{16,8},{24,0},{1,25},{9,17},{17,9},{25,1},{2,26},{10... | collective-permute-start | bytes 3145736 | tf_op jit(solution)/shard_map/ppermute | solution.py:499
  100.5 0.1 broadcast_in_dim.29
  100.6 0.1 convert_element_type.28.frame_ref
  100.7 0.6 gather_fusion.2
  101.3 0.3 collective-permute-start.4
  101.6 0.1 collective-permute-start.5
  101.7 1.6 far_sums.5
  103.3 4.3 %far_sums.4 = f32[2,832]{1,0:T(2,128)S(1)} custom-call(bf16[2,20,208,128]{3,2,1,0:T(8,128)(2,1)S(1)} %copy-done.1, bf16[2,20,208,128]{3,2,1,0:T(8,128)(2,1)S(1)} %copy-done.1, bf16[2,20,208,128]{3,2,1,0:T(8,128)(2,1)} %collective-permute-done.refs_2_.refs_3_.rest_2_.rest_3_, bf16[2,20,208,128]{3,2,1,0:T(8,128)(2,1)} %collective-permute-done.refs_2_.refs_3_.rest_2_.rest_3_, ...), custom_call_target="tpu_custom_call" | custom-call | flops 6815744 | bytes 6815744 | tf_op jit(solution)/shard_map/far_sums/pallas_call | solution.py:280
  107.6 4.9 %psum.22 = f32[2,832]{1,0:T(2,128)S(1)} all-reduce(f32[2,832]{1,0:T(2,128)S(1)} %add.121), channel_id=1, replica_groups=mesh['tm'=4,'space'=2,'dp'=4] {'space'}, use_global_device_ids=true, to_apply=%region_1.0 | all-reduce | flops 1664 | bytes 13312 | tf_op jit(solution)/shard_map/psum | solution.py:344
  112.6 14.4 %temporal_weights.4.rest_4_ = bf16[16,13,64,64]{3,2,1,0:T(8,128)(2,1)} custom-call(s32[4]{0:T(128)S(1)} %iota_xor_fusion.slots_ref, s32[8,128]{1,0:T(8,128)S(1)} %bitcast.51, f32[2,896]{1,0:T(2,128)S(1)} %pad.8.factor_ref, f32[1,64]{1,0:T(1,128)S(1)} %convert_element_type.28.frame_ref, f32[20,1,128]{2,1,0:T(1,128)S(1)} %broadcast_in_dim.27.qg_ref, ...), custom_call_target="tpu_custom_call" | custom-call | flops 218103808 | bytes 8519680 | tf_op jit(solution)/shard_map/temporal_weights/pallas_call | solution.py:358
  127.0 1.2 collective-permute-start.6
  128.2 0.1 reduce_sum.9
  128.4 0.7 reduce_max.9
  129.7 0.6 gather_fusion.3
  130.4 1.6 conditional.1
  130.7 1.3 broadcast_in_dim.4
  132.0 0.1 add_xor_fusion
  132.0 0.1 pad_add_fusion.slots_ref
  132.1 1.0 copy-done.7
  133.1 4.4 %temporal_weights.5.rest_4_ = bf16[4,13,64,64]{3,2,1,0:T(8,128)(2,1)S(1)} custom-call(s32[4]{0:T(128)S(1)} %iota_xor_fusion.slots_ref, s32[8,128]{1,0:T(8,128)S(1)} %bitcast.53, f32[2,896]{1,0:T(2,128)S(1)} %pad.8.factor_ref, f32[1,64]{1,0:T(1,128)S(1)} %convert_element_type.28.frame_ref, f32[20,1,128]{2,1,0:T(1,128)S(1)} %broadcast_in_dim.27.qg_ref, ...), custom_call_target="tpu_custom_call" | custom-call | flops 54525952 | bytes 2129920 | tf_op jit(solution)/shard_map/temporal_weights/pallas_call | solution.py:358
  137.5 4.9 %collective-permute-done.9.rest_3_ = bf16[16,256,128]{2,1,0:T(8,128)(2,1)} collective-permute-done((bf16[16,256,128]{2,1,0:T(8,128)(2,1)}, bf16[16,256,128]{2,1,0:T(8,128)(2,1)}, u32[]{:S(2)}, u32[]{:S(2)}) %collective-permute-start.9) | collective-permute-done | bytes 1048608 | tf_op jit(solution)/shard_map/ppermute | solution.py:499
  142.4 6.7 %temporal_mix.2 = (f32[2,512]{1,0:T(2,128)S(1)}, f32[2,512]{1,0:T(2,128)S(1)}, f32[2,512]{1,0:T(2,128)S(1)}, f32[2,512]{1,0:T(2,128)S(1)}) custom-call(s32[8]{0:T(128)S(1)} %pad_add_fusion.slots_ref, s32[8,128]{1,0:T(8,128)S(1)} %bitcast.54, f32[20,4,128]{2,1,0:T(4,128)S(1)} %bitcast.31, f32[20,1,128]{2,1,0:T(1,128)S(1)} %broadcast_in_dim.26.weight_ref, ...), custom_call_target="tpu_custom_call" | custom-call | flops 268435456 | bytes 6291456 | tf_op jit(solution)/shard_map/temporal_mix/pallas_call | solution.py:448
  149.2 0.1 collective-permute-done.5.rest_2_
  149.3 4.3 %collective-permute-done.6.rest_3_ = bf16[4,256,128]{2,1,0:T(8,128)(2,1)} collective-permute-done((bf16[4,256,128]{2,1,0:T(8,128)(2,1)}, bf16[4,256,128]{2,1,0:T(8,128)(2,1)}, u32[]{:S(2)}, u32[]{:S(2)}) %collective-permute-start.6) | collective-permute-done | bytes 262176 | tf_op jit(solution)/shard_map/ppermute | solution.py:499
  153.7 3.0 %temporal_mix.3 = (f32[2,512]{1,0:T(2,128)S(1)}, f32[2,512]{1,0:T(2,128)S(1)}, f32[2,512]{1,0:T(2,128)S(1)}, f32[2,512]{1,0:T(2,128)S(1)}) custom-call(s32[8]{0:T(128)S(1)} %pad_add_fusion.slots_ref, s32[8,128]{1,0:T(8,128)S(1)} %bitcast.55, f32[20,4,128]{2,1,0:T(4,128)S(1)} %bitcast.32, f32[20,1,128]{2,1,0:T(1,128)S(1)} %broadcast_in_dim.26.weight_ref, ...), custom_call_target="tpu_custom_call" | custom-call | flops 67108864 | bytes 1572864 | tf_op jit(solution)/shard_map/temporal_mix/pallas_call | solution.py:448
  156.6 4.5 %collective-permute-start.10 = (f32[2,512]{1,0:T(2,128)S(1)}, f32[2,512]{1,0:T(2,128)S(1)}, u32[]{:S(2)}, u32[]{:S(2)}) collective-permute-start(f32[2,512]{1,0:T(2,128)S(1)} %get-tuple-element.88), channel_id=1, source_target_pairs={{0,0},{16,4},{8,8},{24,12},{4,16},{20,20},{12,24},{28,28},{1,1},{1... | collective-permute-start | bytes 12296 | tf_op jit(solution)/shard_map/ppermute | solution.py:601
  161.1 0.0 collective-permute-start.11
  161.1 1.0 collective-permute-start.12
  162.1 1.0 collective-permute-start.13
  163.2 0.4 collective-permute-done.11
  163.6 1.5 collective-permute-done.12
  165.1 0.4 collective-permute-done.13
  165.5 0.6 fusion.10
  (46 shorter events, 0.2 us)
Async XLA Ops:
  0.0 129.7 %copy-start = (f32[4,20,128]{2,0,1:T(4,128)S(1)}, f32[4,20,128]{2,0,1:T(4,128)}, u32[]{:S(2)}) copy-start(f32[4,20,128]{2,0,1:T(4,128)} %param.13) | copy-start | bytes 122884
  0.0 5.6 %copy-start.11 = (s32[1024]{0:T(1024)S(1)}, s32[1024]{0:T(1024)}, u32[]{:S(2)}) copy-start(s32[1024]{0:T(1024)} %param.15) | copy-start | bytes 12292
  2.5 65.3 %collective-permute-start.2 = (bf16[2,4,208,128]{3,2,1,0:T(8,128)(2,1)S(1)}, bf16[2,4,208,128]{3,2,1,0:T(8,128)(2,1)S(1)}, u32[]{:S(2)}, u32[]{:S(2)}) collective-permute-start(bf16[2,4,208,128]{3,2,1,0:T(8,128)(2,1)S(1)} %gather.29), channel_id=1, source_target_pairs={{0,24},{8,16},{16,8},{24,0},{1,25},{9,17},{17,9},{25,1},{2,26},{10... | collective-permute-start | bytes 1277960 | tf_op jit(solution)/shard_map/ppermute | solution.py:499
  11.3 14.9 %copy-start.12 = (f32[20,128]{1,0:T(8,128)S(1)}, f32[20,128]{1,0:T(8,128)}, u32[]{:S(2)}) copy-start(f32[20,128]{1,0:T(8,128)} %param.10) | copy-start | bytes 30724
  11.3 14.9 %copy-start.13 = (f32[20,128]{1,0:T(8,128)S(1)}, f32[20,128]{1,0:T(8,128)}, u32[]{:S(2)}) copy-start(f32[20,128]{1,0:T(8,128)} %param.11) | copy-start | bytes 30724
  11.3 68.7 %collective-permute-start.3 = (bf16[2,16,208,128]{3,2,1,0:T(8,128)(2,1)}, bf16[2,16,208,128]{3,2,1,0:T(8,128)(2,1)}, u32[]{:S(2)}, u32[]{:S(2)}) collective-permute-start(bf16[2,16,208,128]{3,2,1,0:T(8,128)(2,1)} %gather.30), channel_id=1, source_target_pairs={{0,24},{8,16},{16,8},{24,0},{1,25},{9,17},{17,9},{25,1},{2,26},{10... | collective-permute-start | bytes 5111816 | tf_op jit(solution)/shard_map/ppermute | solution.py:499
  23.6 73.8 %collective-permute-start = (bf16[2,20,208,128]{3,2,1,0:T(8,128)(2,1)}, bf16[2,20,208,128]{3,2,1,0:T(8,128)(2,1)}, u32[]{:S(2)}, u32[]{:S(2)}) collective-permute-start(bf16[2,20,208,128]{3,2,1,0:T(8,128)(2,1)} %get-tuple-element.65), channel_id=1, source_target_pairs={{0,8},{8,0},{16,24},{24,16},{1,9},{9,1},{17,25},{25,17},{2,10},{10... | collective-permute-start | bytes 6389768 | tf_op jit(solution)/shard_map/ppermute | solution.py:499
  25.0 73.2 %collective-permute-start.1 = (bf16[2,20,208,128]{3,2,1,0:T(8,128)(2,1)}, bf16[2,20,208,128]{3,2,1,0:T(8,128)(2,1)}, u32[]{:S(2)}, u32[]{:S(2)}) collective-permute-start(bf16[2,20,208,128]{3,2,1,0:T(8,128)(2,1)} %get-tuple-element.66), channel_id=1, source_target_pairs={{0,16},{8,24},{16,0},{24,8},{1,17},{9,25},{17,1},{25,9},{2,18},{10... | collective-permute-start | bytes 6389768 | tf_op jit(solution)/shard_map/ppermute | solution.py:499
  66.9 1.0 copy-start.8
  67.9 33.8 %copy-start.6 = (bf16[2,4,208,128]{3,2,1,0:T(8,128)(2,1)}, bf16[2,4,208,128]{3,2,1,0:T(8,128)(2,1)S(1)}, u32[]{:S(2)}) copy-start(bf16[2,4,208,128]{3,2,1,0:T(8,128)(2,1)S(1)} %collective-permute-done.2.refs_6_.refs_7_.rest_6_.rest_7_) | copy-start | bytes 1277956
  67.9 32.8 %copy-start.10 = (s32[4]{0:T(128)S(1)}, s32[4]{0:T(128)}, u32[]{:S(2)}) copy-start(s32[4]{0:T(128)} %param.14) | copy-start | bytes 52
  67.9 59.1 %collective-permute-start.8 = (bf16[16,256,128]{2,1,0:T(8,128)(2,1)}, bf16[16,256,128]{2,1,0:T(8,128)(2,1)}, u32[]{:S(2)}, u32[]{:S(2)}) collective-permute-start(bf16[16,256,128]{2,1,0:T(8,128)(2,1)} %get-tuple-element.81), channel_id=1, source_target_pairs={{0,16},{8,24},{16,0},{24,8},{1,17},{9,25},{17,1},{25,9},{2,18},{10... | collective-permute-start | bytes 3145736 | tf_op jit(solution)/shard_map/ppermute | solution.py:499
  68.1 33.6 %copy-start.1 = (bf16[2,20,208,128]{3,2,1,0:T(8,128)(2,1)S(1)}, bf16[2,20,208,128]{3,2,1,0:T(8,128)(2,1)}, u32[]{:S(2)}) copy-start(bf16[2,20,208,128]{3,2,1,0:T(8,128)(2,1)} %get-tuple-element.75.refs_0_.refs_1_.rest_0_.rest_1_) | copy-start | bytes 6389764
  79.8 57.7 %collective-permute-start.7 = (bf16[16,256,128]{2,1,0:T(8,128)(2,1)}, bf16[16,256,128]{2,1,0:T(8,128)(2,1)}, u32[]{:S(2)}, u32[]{:S(2)}) collective-permute-start(bf16[16,256,128]{2,1,0:T(8,128)(2,1)} %get-tuple-element.79), channel_id=1, source_target_pairs={{0,8},{8,0},{16,24},{24,16},{1,9},{9,1},{17,25},{25,17},{2,10},{10... | collective-permute-start | bytes 3145736 | tf_op jit(solution)/shard_map/ppermute | solution.py:499
  98.1 44.3 %collective-permute-start.9 = (bf16[16,256,128]{2,1,0:T(8,128)(2,1)}, bf16[16,256,128]{2,1,0:T(8,128)(2,1)}, u32[]{:S(2)}, u32[]{:S(2)}) collective-permute-start(bf16[16,256,128]{2,1,0:T(8,128)(2,1)} %get-tuple-element.83), channel_id=1, source_target_pairs={{0,24},{8,16},{16,8},{24,0},{1,25},{9,17},{17,9},{25,1},{2,26},{10... | collective-permute-start | bytes 3145736 | tf_op jit(solution)/shard_map/ppermute | solution.py:499
  101.3 47.9 %collective-permute-start.4 = (bf16[4,256,128]{2,1,0:T(8,128)(2,1)}, bf16[4,256,128]{2,1,0:T(8,128)(2,1)}, u32[]{:S(2)}, u32[]{:S(2)}) collective-permute-start(bf16[4,256,128]{2,1,0:T(8,128)(2,1)} %get-tuple-element.71), channel_id=1, source_target_pairs={{0,8},{8,0},{16,24},{24,16},{1,9},{9,1},{17,25},{25,17},{2,10},{10... | collective-permute-start | bytes 786440 | tf_op jit(solution)/shard_map/ppermute | solution.py:499
  101.6 47.7 %collective-permute-start.5 = (bf16[4,256,128]{2,1,0:T(8,128)(2,1)}, bf16[4,256,128]{2,1,0:T(8,128)(2,1)}, u32[]{:S(2)}, u32[]{:S(2)}) collective-permute-start(bf16[4,256,128]{2,1,0:T(8,128)(2,1)} %get-tuple-element.73), channel_id=1, source_target_pairs={{0,16},{8,24},{16,0},{24,8},{1,17},{9,25},{17,1},{25,9},{2,18},{10... | collective-permute-start | bytes 786440 | tf_op jit(solution)/shard_map/ppermute | solution.py:499
  112.6 17.1 %copy-start.14 = (f32[20,128]{1,0:T(8,128)S(1)}, f32[20,128]{1,0:T(8,128)}, u32[]{:S(2)}) copy-start(f32[20,128]{1,0:T(8,128)} %param.12) | copy-start | bytes 30724
  127.0 26.7 %collective-permute-start.6 = (bf16[4,256,128]{2,1,0:T(8,128)(2,1)}, bf16[4,256,128]{2,1,0:T(8,128)(2,1)}, u32[]{:S(2)}, u32[]{:S(2)}) collective-permute-start(bf16[4,256,128]{2,1,0:T(8,128)(2,1)} %get-tuple-element.76), channel_id=1, source_target_pairs={{0,24},{8,16},{16,8},{24,0},{1,25},{9,17},{17,9},{25,1},{2,26},{10... | collective-permute-start | bytes 786440 | tf_op jit(solution)/shard_map/ppermute | solution.py:499
  132.1 1.0 copy-start.7
  133.1 9.3 %copy-start.9 = (bf16[16,256,128]{2,1,0:T(8,128)(2,1)S(1)}, bf16[16,256,128]{2,1,0:T(8,128)(2,1)}, u32[]{:S(2)}) copy-start(bf16[16,256,128]{2,1,0:T(8,128)(2,1)} %copy-done.8) | copy-start | bytes 3145732
  156.6 6.5 %collective-permute-start.10 = (f32[2,512]{1,0:T(2,128)S(1)}, f32[2,512]{1,0:T(2,128)S(1)}, u32[]{:S(2)}, u32[]{:S(2)}) collective-permute-start(f32[2,512]{1,0:T(2,128)S(1)} %get-tuple-element.88), channel_id=1, source_target_pairs={{0,0},{16,4},{8,8},{24,12},{4,16},{20,20},{12,24},{28,28},{1,1},{1... | collective-permute-start | bytes 12296 | tf_op jit(solution)/shard_map/ppermute | solution.py:601
  161.1 2.5 %collective-permute-start.11 = (f32[2,512]{1,0:T(2,128)S(1)}, f32[2,512]{1,0:T(2,128)S(1)}, u32[]{:S(2)}, u32[]{:S(2)}) collective-permute-start(f32[2,512]{1,0:T(2,128)S(1)} %get-tuple-element.89), channel_id=1, source_target_pairs={{4,0},{20,4},{12,8},{28,12},{0,16},{16,20},{8,24},{24,28},{5,1},{2... | collective-permute-start | bytes 12296 | tf_op jit(solution)/shard_map/ppermute | solution.py:601
  161.1 4.0 %collective-permute-start.12 = (f32[2,512]{1,0:T(2,128)S(1)}, f32[2,512]{1,0:T(2,128)S(1)}, u32[]{:S(2)}, u32[]{:S(2)}) collective-permute-start(f32[2,512]{1,0:T(2,128)S(1)} %get-tuple-element.90), channel_id=1, source_target_pairs={{8,0},{24,4},{0,8},{16,12},{12,16},{28,20},{4,24},{20,28},{9,1},{2... | collective-permute-start | bytes 12296 | tf_op jit(solution)/shard_map/ppermute | solution.py:601
  162.1 3.4 %collective-permute-start.13 = (f32[2,512]{1,0:T(2,128)S(1)}, f32[2,512]{1,0:T(2,128)S(1)}, u32[]{:S(2)}, u32[]{:S(2)}) collective-permute-start(f32[2,512]{1,0:T(2,128)S(1)} %get-tuple-element.91), channel_id=1, source_target_pairs={{12,0},{28,4},{4,8},{20,12},{8,16},{24,20},{0,24},{16,28},{13,1},{... | collective-permute-start | bytes 12296 | tf_op jit(solution)/shard_map/ppermute | solution.py:601

commit v2 on v1

--- a/solution.py
+++ b/solution.py
@@ -164,6 +164,71 @@
         ),
         name="gather_sums" if with_sums else "gather",
     )(slots, counts, *[x] * (len(in_specs) - 1))
+
+
+def first_kernel(slots_ref, count_ref, x_ref, out_ref, rank_ref, held_ref, sems, *, offset, each, at):
+    width = held_ref.shape[2]
+    owner = slots_ref[offset]
+    start = pl.multiple_of(lax.div(owner, each) * width, width)
+    copies = [
+        [
+            pltpu.make_async_copy(
+                x_ref.at[which, at + h, pl.ds(start, width)],
+                held_ref.at[which, h],
+                sems.at[which, h],
+            )
+            for which in range(2)
+        ]
+        for h in range(held_ref.shape[1])
+    ]
+    for pair in copies:
+        for copy in pair:
+            copy.start()
+    store_shares(count_ref, rank_ref)
+    hit = picks(rank_ref, owner, each, 0, out_ref.shape[2])
+    hit = jnp.where(hit, 1.0, 0.0).astype(jnp.bfloat16)
+    for h, pair in enumerate(copies):
+        for copy in pair:
+            copy.wait()
+        rows = jnp.concatenate([held_ref[0, h], held_ref[1, h]], axis=1)
+        rows = jnp.dot(hit, rows, preferred_element_type=jnp.float32).astype(jnp.bfloat16)
+        out_ref[0, h] = rows[:, :HEAD]
+        out_ref[1, h] = rows[:, HEAD:]
+
+
+def gather_first(slots, counts, x, offset, each, shares, size, at, heads):
+    pixels = x.shape[2]
+    width = pixels // shares
+    return pl.pallas_call(
+        functools.partial(first_kernel, offset=offset, each=each, at=at),
+        grid_spec=pltpu.PrefetchScalarGridSpec(
+            num_scalar_prefetch=1,
+            grid=(1,),
+            in_specs=[
+                pl.BlockSpec(counts.shape, lambda h, s: (0, 0)),
+                pl.BlockSpec(memory_space=pl.ANY),
+            ],
+            out_specs=[
+                pl.BlockSpec((2, heads, size, HEAD), lambda h, s: (0, 0, 0, 0)),
+                pl.BlockSpec((shares, width), lambda h, s: (0, 0)),
+            ],
+            scratch_shapes=[
+                pltpu.VMEM((2, heads, width, HEAD), jnp.bfloat16),
+                pltpu.SemaphoreType.DMA((2, heads)),
+            ],
+        ),
+        out_shape=[
+            jax.ShapeDtypeStruct((2, heads, size, HEAD), jnp.bfloat16),
+            jax.ShapeDtypeStruct((shares, width), jnp.int32),
+        ],
+        compiler_params=pltpu.CompilerParams(vmem_limit_bytes=VMEM_LIMIT),
+        cost_estimate=pl.CostEstimate(
+            flops=4 * heads * pixels * HEAD,
+            bytes_accessed=4 * heads * (size + pixels) * HEAD,
+            transcendentals=0,
+        ),
+        name="gather_first",
+    )(slots, counts, x)
 
 
 def spatial_kernel(
@@ -301,7 +366,8 @@
 def weights_kernel(
     slots_ref, count_ref, factor_ref, frame_ref, qg_ref, kg_ref, *rest, each, first, part
 ):
-    far, (out_ref, fq_ref, fk_ref, rank_ref, frames_ref, bias_ref) = rest[:-6], rest[-6:]
+    far, rest = rest[:-7], rest[-7:]
+    out_ref, fq_ref, fk_ref, rank_ref, frames_ref, bias_ref, unit_ref = rest
     count = len(far) // 2
     size = far[0].shape[2]
     wide = count * part
@@ -315,9 +381,10 @@
         frames = frames_ref[pl.ds(lax.div(me, each), 1), :]
         hit = picks(rank_ref, me, each, first, size)
         frames = jnp.sum(jnp.where(hit, frames, 0.0), axis=1, keepdims=True)
-        row = lax.broadcasted_iota(jnp.int32, (wide, wide), 0)
-        column = lax.broadcasted_iota(jnp.int32, (wide, wide), 1)
-        same = ((row - column) & (part - 1)) == 0
+        row = lax.broadcasted_iota(jnp.int32, (wide, 2 * wide), 0)
+        column = lax.broadcasted_iota(jnp.int32, (wide, 2 * wide), 1)
+        same = (((row - column) & (part - 1)) == 0) & (column < wide)
+        unit_ref[...] = jnp.where(column - row == wide, 1.0, 0.0)
         for j in range(size // part):
             held = jnp.concatenate([frames[j * part : (j + 1) * part]] * count, axis=0)
             live = jnp.where(frame_ref[...] < held, 0.0, MASKED)
@@ -334,9 +401,11 @@
     for j in range(size // part):
         qn = normal(0, fq_ref, qg_ref[0], j * part)
         kn = normal(1, fk_ref, kg_ref[0], j * part)
+        kn = jnp.concatenate([kn, kn], axis=0)
         s = lax.dot_general(qn, kn, NT, preferred_element_type=jnp.float32) * SCALE2 + bias_ref[j]
         e = jnp.exp2(s - jnp.max(s, axis=1, keepdims=True))
-        out_ref[0, j] = (e * (1.0 / jnp.sum(e, axis=1, keepdims=True))).astype(jnp.bfloat16)
+        p = e * (1.0 / jnp.sum(e, axis=1, keepdims=True)) + unit_ref[...]
+        out_ref[0, j] = p.astype(jnp.bfloat16)
 
 
 def position_factors(parts):
@@ -353,7 +422,7 @@
     rows, wide, subs = count * size, count * part, size // part
     width = counts.size // shares
     padded = factors.shape[1]
-    frame = jnp.repeat(slots, part)[None, :].astype(jnp.float32)
+    frame = jnp.tile(jnp.repeat(slots, part), 2)[None, :].astype(jnp.float32)
     gain = pl.BlockSpec((1, 1, HEAD), lambda h, s: (start + h, 0, 0))
     return pl.pallas_call(
         functools.partial(weights_kernel, each=each, first=first, part=part),
@@ -363,7 +432,7 @@
             in_specs=[
                 pl.BlockSpec(counts.shape, lambda h, s: (0, 0)),
                 pl.BlockSpec((2, padded), lambda h, s: (0, 0)),
-                pl.BlockSpec((1, wide), lambda h, s: (0, 0)),
+                pl.BlockSpec((1, 2 * wide), lambda h, s: (0, 0)),
                 gain,
                 gain,
             ]
@@ -373,16 +442,17 @@
                 )
                 for _, place, at in far
             ],
-            out_specs=pl.BlockSpec((1, subs, wide, wide), lambda h, s: (h, 0, 0, 0)),
+            out_specs=pl.BlockSpec((1, subs, wide, 2 * wide), lambda h, s: (h, 0, 0, 0)),
             scratch_shapes=[
                 pltpu.VMEM((padded, HEAD), jnp.float32),
                 pltpu.VMEM((padded, HEAD), jnp.float32),
                 pltpu.VMEM((shares, width), jnp.int32),
                 pltpu.VMEM((shares, width), jnp.float32),
-                pltpu.VMEM((subs, wide, wide), jnp.float32),
+                pltpu.VMEM((subs, wide, 2 * wide), jnp.float32),
+                pltpu.VMEM((wide, 2 * wide), jnp.float32),
             ],
         ),
-        out_shape=jax.ShapeDtypeStruct((heads, subs, wide, wide), jnp.bfloat16),
+        out_shape=jax.ShapeDtypeStruct((heads, subs, wide, 2 * wide), jnp.bfloat16),
         compiler_params=pltpu.CompilerParams(vmem_limit_bytes=VMEM_LIMIT),
         cost_estimate=pl.CostEstimate(
             flops=2 * heads * rows * wide * HEAD,
@@ -393,29 +463,35 @@
     )(slots, counts, factors, frame, q_gain, k_gain, *[array for array, _, _ in far])
 
 
-def mix_kernel(slots_ref, count_ref, scale_ref, weight_ref, *rest, count, each, part, more):
+def mix_kernel(
+    slots_ref, rank_ref, scale_ref, weight_ref, *rest, count, each, shares, part, more, single
+):
     mixed, rest = rest[:count], rest[count:]
-    weights, rest = rest[: -(count + 3 + more * count)], rest[-(count + 3 + more * count) :]
-    before, rest = rest[: more * count], rest[more * count :]
-    outs, (dot_ref, square_ref, rank_ref) = rest[:count], rest[count:]
+    weights, rest = rest[: -(2 + (1 + more) * shares)], rest[-(2 + (1 + more) * shares) :]
+    before, outs, (dot_ref, square_ref) = rest[: more * shares], rest[more * shares : -2], rest[-2:]
     head = pl.program_id(0)
     block = mixed[0].shape[1]
 
-    @pl.when(head == 0)
-    def _():
-        dot_ref[...] = jnp.zeros_like(dot_ref)
-        square_ref[...] = jnp.zeros_like(square_ref)
-        store_shares(count_ref, rank_ref)
+    if not single:
+
+        @pl.when(head == 0)
+        def _():
+            dot_ref[...] = jnp.zeros_like(dot_ref)
+            square_ref[...] = jnp.zeros_like(square_ref)
 
     subs = [(ref, j) for ref in weights for j in range(ref.shape[1])]
     for sub, (p_ref, j) in enumerate(subs):
         at = sub * part
-        dots = [dot_ref[slot, at : at + part] for slot in range(count)]
-        squares = [square_ref[slot, at : at + part] for slot in range(count)]
+        if single:
+            dots = [jnp.zeros((part, HEAD), jnp.float32)] * count
+            squares = list(dots)
+        else:
+            dots = [dot_ref[slot, at : at + part] for slot in range(count)]
+            squares = [square_ref[slot, at : at + part] for slot in range(count)]
         for h in range(p_ref.shape[0]):
             o = jnp.concatenate([mixed[slot][h, at : at + part] for slot in range(count)], axis=0)
-            t = jnp.dot(p_ref[h, j], o, preferred_element_type=jnp.float32).astype(jnp.bfloat16)
-            both = o.astype(jnp.float32) + t.astype(jnp.float32)
+            o = jnp.concatenate([o, o], axis=0)
+            both = jnp.dot(p_ref[h, j], o, preferred_element_type=jnp.float32)
             for slot in range(count):
                 m = both[slot * part : (slot + 1) * part] * scale_ref[h, slot : slot + 1]
                 dots[slot] = dots[slot] + m * weight_ref[h]
@@ -427,31 +503,40 @@
     @pl.when(head == pl.num_programs(0) - 1)
     def _():
         hit = picks(rank_ref, slots_ref[0], each, 0, block)
-        for i, out in enumerate(outs):
+        for i in range(count):
+            share, r = i // each, i % each
             for which, ref in enumerate((dot_ref, square_ref)):
                 sums = jnp.sum(ref[slots_ref[count + i]], axis=1, keepdims=True)
                 sums = jnp.sum(jnp.where(hit, sums, 0.0), axis=0, keepdims=True)
                 if more:
-                    sums = before[i][which : which + 1] + sums
-                out[which : which + 1] = sums
-
-
-def mix(slots, counts, weights, scales, weight, before, mixed, first, each, shares, part):
+                    sums = before[share][r, which : which + 1] + sums
+                outs[share][r, which : which + 1] = sums
+
+
+def mix(slots, ranks, weights, scales, weight, before, mixed, first, each, shares, part):
     count = len(mixed)
     size, block, _ = mixed[0].shape
     wide = count * part
     rows = count * block
-    width = counts.size // shares
+    width = ranks.shape[1]
     step = max(i for i in range(1, 6) if size % i == 0 and first % i == 0)
     skip = first // step
-    out = pl.BlockSpec((2, width), lambda h, s: (0, 0))
+    out = pl.BlockSpec((each, 2, width), lambda h, s: (0, 0, 0))
     return pl.pallas_call(
-        functools.partial(mix_kernel, count=count, each=each, part=part, more=len(before) // count),
+        functools.partial(
+            mix_kernel,
+            count=count,
+            each=each,
+            shares=shares,
+            part=part,
+            more=len(before) // shares,
+            single=size == step,
+        ),
         grid_spec=pltpu.PrefetchScalarGridSpec(
             num_scalar_prefetch=1,
             grid=(size // step,),
             in_specs=[
-                pl.BlockSpec(counts.shape, lambda h, s: (0, 0)),
+                pl.BlockSpec(ranks.shape, lambda h, s: (0, 0)),
                 pl.BlockSpec((step, count, HEAD), lambda h, s: (skip + h, 0, 0)),
                 pl.BlockSpec((step, 1, HEAD), lambda h, s: (skip + h, 0, 0)),
             ]
@@ -464,14 +549,13 @@
                 for p, at in weights
             ]
             + [out] * len(before),
-            out_specs=[out] * count,
+            out_specs=[out] * shares,
             scratch_shapes=[
                 pltpu.VMEM((count, block, HEAD), jnp.float32),
                 pltpu.VMEM((count, block, HEAD), jnp.float32),
-                pltpu.VMEM((shares, width), jnp.int32),
             ],
         ),
-        out_shape=[jax.ShapeDtypeStruct((2, width), jnp.float32)] * count,
+        out_shape=[jax.ShapeDtypeStruct((each, 2, width), jnp.float32)] * shares,
         compiler_params=pltpu.CompilerParams(vmem_limit_bytes=VMEM_LIMIT),
         cost_estimate=pl.CostEstimate(
             flops=2 * size * rows * wide * HEAD,
@@ -479,7 +563,7 @@
             transcendentals=0,
         ),
         name="temporal_mix",
-    )(slots, counts, scales, weight, *mixed, *[p for p, _ in weights], *before)
+    )(slots, ranks, scales, weight, *mixed, *[p for p, _ in weights], *before)
 
 
 def on_device(
@@ -503,7 +587,12 @@
     diagonal = {}
     after = slots
     for at, size in reversed(ranges):
-        (piece,) = gather(after, counts, x, [count - 1], each, shares, 0, sure, at, size)
+        if after is slots:
+            piece, ranks = gather_first(
+                after, counts, x, count - 1, each, shares, sure, at, size
+            )
+        else:
+            (piece,) = gather(after, counts, x, [count - 1], each, shares, 0, sure, at, size)
         diagonal[at] = swap(piece, count - 1)
         after = lax.optimization_barrier((slots, piece))[0]
     near = range(1, count - 1)
@@ -558,11 +647,12 @@
 
         def single():
             wide = count * part
-            row = lax.broadcasted_iota(jnp.int32, (wide, wide), 0)
-            column = lax.broadcasted_iota(jnp.int32, (wide, wide), 1)
+            row = lax.broadcasted_iota(jnp.int32, (wide, 2 * wide), 0)
+            column = lax.broadcasted_iota(jnp.int32, (wide, 2 * wide), 1)
             hit = ((row - column) % part == 0) & (column // part == me)
+            hit = hit | (column - row == wide)
             return jnp.broadcast_to(
-                hit.astype(jnp.bfloat16), (heads, (block - sure) // part, wide, wide)
+                hit.astype(jnp.bfloat16), (heads, (block - sure) // part, wide, 2 * wide)
             )
 
         others = lax.cond(crowd > float(sure * each), exchanged, single)
@@ -577,30 +667,30 @@
         outs[offset] = lax.optimization_barrier((outs[offset], *after))[0]
 
     core = lax.axis_index("space")
-    rounds = [(r, u) for r in range(each) for u in range(shares)]
-    frames = [(core - u) % shares * each + (me - r) % each for r, u in rounds]
+    frames = [
+        (core - u) % shares * each + (me - r) % each for u in range(shares) for r in range(each)
+    ]
     order = jnp.concatenate([slots, me ^ jnp.stack(frames)])
     total = []
     for at, outs in groups:
         mixed = [outs[0]] + [swap(outs[offset], offset) for offset in range(1, count)]
         total = mix(
-            order, counts, weights[at], scales, weight, total, mixed, at, each, shares, part
+            order, ranks, weights[at], scales, weight, total, mixed, at, each, shares, part
         )
-    logits = jnp.zeros((width,), jnp.float32)
+    sums = total[0]
+    for u in range(1, shares):
+        turn = [(c, (c - u) % shares) for c in range(shares)]
+        sums = sums + lax.ppermute(total[u], "space", turn)
+    logits = sums[:, 0] * lax.rsqrt(sums[:, 1] / CHANNELS + EPSILON)
+    mine = jnp.zeros((width,), jnp.float32)
     for r in range(each):
-        sums = jnp.zeros((2, width), jnp.float32)
-        for u in range(shares):
-            pairs = [
-                (
-                    (s * each + (f + r) % each) * shares + (f // each + u) % shares,
-                    f * shares + s,
-                )
-                for f in range(count)
-                for s in range(shares)
-            ]
-            sums = sums + lax.ppermute(total[r * shares + u], ("tm", "space"), pairs)
-        logits = logits + sums[0] * lax.rsqrt(sums[1] / CHANNELS + EPSILON)
-    return logits[None, :]
+        pairs = [
+            ((s * each + (f + r) % each) * shares + f // each, f * shares + s)
+            for f in range(count)
+            for s in range(shares)
+        ]
+        mine = mine + lax.ppermute(logits[r], ("tm", "space"), pairs)
+    return mine[None, :]
 
 
 def solution(mesh):

time: 168 us -> 169 us (level)
  Pallas kernels: 103 us -> 105 us
    pallas_call x2 -> x3, Pallas kernels: 9.71 us -> 12.6 us  [the longest x2 9.28 us: mix(): pl.pallas_call(functools.partial(mix_kernel, count=count, each=each, shar...]
    pallas_call x3 -> x2, Pallas kernels: 20.5 us -> 18 us  [gather(): pl.pallas_call(functools.partial(gather_kernel, offsets=tuple(offsets), e...]
    ppermute x4 -> x3, waiting for transfers between devices: 2.33 us -> 3.53 us  [the longest x2 2.71 us: on_device(): mine = mine + lax.ppermute(logits[r], ('tm', 'space'), pairs)]
    ppermute x4 -> x3, starting transfers between devices: 6.5 us -> 6.13 us  [the longest x2 4.84 us: on_device(): mine = mine + lax.ppermute(logits[r], ('tm', 'space'), pairs)]
  transfers between devices with their start and end apart: 14 -> 13, of which waited for: 8 -> 8; matrix products, arithmetic and copies ran while one was open for 2% -> 2% of each run, Pallas kernels for 59% -> 59%
where the time goes in v2:
time: 169 us; the launch traced here: 168 us
  Pallas kernels  105 us (62%)
  waiting for transfers between devices  29.7 us (18%)
  starting transfers between devices  16.3 us (10%)
  blocking collectives  8.83 us (5%)
  local copies, waits for them, and re-layouts  4.9 us (3%)
    pallas_call x2, Pallas kernels, spatial(): pl.pallas_call(functools.partial(spatial_kernel, count=count, each=each),...  48.4 us
    ppermute x10, waiting for transfers between devices, swap(): return lax.ppermute(value, 'tm', [(i, i ^ offset) for i in range(count)])  26.2 us
    pallas_call x2, Pallas kernels, temporal_weights(): pl.pallas_call(functools.partial(weights_kernel, each=each, first=first,...  20.3 us
    pallas_call x2, Pallas kernels, gather(): pl.pallas_call(functools.partial(gather_kernel, offsets=tuple(offsets), e...  18 us
    ppermute x10, starting transfers between devices, swap(): return lax.ppermute(value, 'tm', [(i, i ^ offset) for i in range(count)])  10.1 us
    pallas_call x2, Pallas kernels, mix(): pl.pallas_call(functools.partial(mix_kernel, count=count, each=each, shar...  9.28 us
    pallas_call x2, Pallas kernels, far_sums(): pl.pallas_call(far_sums_kernel, grid=(heads // step,), in_specs=[pl.Block...  5.92 us
    psum x1, blocking collectives, position_factors(): factors = lax.rsqrt(lax.psum(sums, 'space') / CHANNELS + EPSILON)  4.91 us
  transfers between devices with their start and end apart: 13, of which 8 were waited for; matrix products, arithmetic and copies ran while one was open for 2% of the time, Pallas kernels for 59%

profile of v2, /device:TPU:1, one launch (start us, length us, event | category | flops | bytes accessed | tf_op | source)
XLA Modules:
  0.0 167.7 jit_solution(8083864720499970375)
XLA Ops:
  0.0 3.3 %gather_first.1 = (bf16[2,4,208,128]{3,2,1,0:T(8,128)(2,1)S(1)}, s32[2,512]{1,0:T(2,128)S(1)}) custom-call(s32[4]{0:T(128)S(1)} %get-tuple-element.61.slots_ref, s32[8,128]{1,0:T(8,128)} %bitcast.48, bf16[3,20,1024,128]{3,2,1,0:T(8,128)(2,1)} %bitcast.36), custom_call_target="tpu_custom_call" | custom-call | flops 2097152 | bytes 2523136 | tf_op jit(solution)/shard_map/gather_first/pallas_call | solution.py:202
  3.3 3.1 %collective-permute-start.2 = (bf16[2,4,208,128]{3,2,1,0:T(8,128)(2,1)S(1)}, bf16[2,4,208,128]{3,2,1,0:T(8,128)(2,1)S(1)}, u32[]{:S(2)}, u32[]{:S(2)}) collective-permute-start(bf16[2,4,208,128]{3,2,1,0:T(8,128)(2,1)S(1)} %get-tuple-element.59), channel_id=1, source_target_pairs={{0,24},{8,16},{16,8},{24,0},{1,25},{9,17},{17,9},{25,1},{2,26},{10... | collective-permute-start | bytes 1277960 | tf_op jit(solution)/shard_map/ppermute | solution.py:583
  6.4 5.7 %gather.28 = bf16[2,16,208,128]{3,2,1,0:T(8,128)(2,1)} custom-call(s32[4]{0:T(128)S(1)} %get-tuple-element.61.slots_ref, s32[8,128]{1,0:T(8,128)S(1)} %bitcast.49, bf16[3,20,1024,128]{3,2,1,0:T(8,128)(2,1)} %bitcast.37, bf16[3,20,1024,128]{3,2,1,0:T(8,128)(2,1)} %bitcast.38), custom_call_target="tpu_custom_call" | custom-call | flops 8388608 | bytes 10092544 | tf_op jit(solution)/shard_map/gather/pallas_call | solution.py:147
  12.1 0.0 collective-permute-start.3
  12.1 12.3 %gather_sums.1 = (bf16[2,20,208,128]{3,2,1,0:T(8,128)(2,1)}, bf16[2,20,208,128]{3,2,1,0:T(8,128)(2,1)}, bf16[2,20,208,128]{3,2,1,0:T(8,128)(2,1)}, f32[2,1024]{1,0:T(2,128)S(1)}) custom-call(s32[4]{0:T(128)S(1)} %get-tuple-element.61.slots_ref, s32[8,128]{1,0:T(8,128)S(1)} %bitcast.50, bf16[3,20,1024,128]{3,2,1,0:T(8,128)(2,1)} %bitcast.39, ...), custom_call_target="tpu_custom_call" | custom-call | flops 10485760 | bytes 16875520 | tf_op jit(solution)/shard_map/gather_sums/pallas_call | solution.py:147
  24.5 1.4 collective-permute-start
  25.9 1.2 collective-permute-start.1
  27.1 3.9 %psum.21 = f32[2,1024]{1,0:T(2,128)S(1)} all-reduce(f32[2,1024]{1,0:T(2,128)S(1)} %get-tuple-element.62), channel_id=1, replica_groups=mesh['tm'=4,'space'=2,'dp'=4] {'space'}, use_global_device_ids=true, to_apply=%region_0.0 | all-reduce | flops 2048 | bytes 16384 | tf_op jit(solution)/shard_map/psum | solution.py:603
  31.1 36.8 %spatial_attention.3 = (bf16[16,256,128]{2,1,0:T(8,128)(2,1)S(1)}, bf16[16,256,128]{2,1,0:T(8,128)(2,1)}, bf16[16,256,128]{2,1,0:T(8,128)(2,1)}, bf16[16,256,128]{2,1,0:T(8,128)(2,1)}) custom-call(s32[4]{0:T(128)S(1)} %get-tuple-element.61.slots_ref, s32[8,128]{1,0:T(8,128)S(1)} %bitcast.51, bf16[3,20,1024,128]{3,2,1,0:T(8,128)(2,1)} %bitcast.41, ...), custom_call_target="tpu_custom_call" | custom-call | flops 17179869184 | bytes 16777216 | tf_op jit(solution)/shard_map/spatial_attention/pallas_call | solution.py:282
  67.9 1.0 copy-done.8
  68.9 0.2 collective-permute-start.8
  69.1 11.7 %spatial_attention.2 = (bf16[4,256,128]{2,1,0:T(8,128)(2,1)S(1)}, bf16[4,256,128]{2,1,0:T(8,128)(2,1)}, bf16[4,256,128]{2,1,0:T(8,128)(2,1)}, bf16[4,256,128]{2,1,0:T(8,128)(2,1)}) custom-call(s32[4]{0:T(128)S(1)} %get-tuple-element.61.slots_ref, s32[8,128]{1,0:T(8,128)S(1)} %bitcast.52, bf16[3,20,1024,128]{3,2,1,0:T(8,128)(2,1)} %bitcast.44, ...), custom_call_target="tpu_custom_call" | custom-call | flops 4294967296 | bytes 4194304 | tf_op jit(solution)/shard_map/spatial_attention/pallas_call | solution.py:282
  80.8 0.3 collective-permute-start.7
  81.1 17.1 %collective-permute-done.refs_2_.refs_3_.rest_2_.rest_3_ = bf16[2,20,208,128]{3,2,1,0:T(8,128)(2,1)} collective-permute-done((bf16[2,20,208,128]{3,2,1,0:T(8,128)(2,1)}, bf16[2,20,208,128]{3,2,1,0:T(8,128)(2,1)}, u32[]{:S(2)}, u32[]{:S(2)}) %collective-permute-start) | collective-permute-done | bytes 2129952 | tf_op jit(solution)/shard_map/ppermute | solution.py:583
  98.2 0.8 collective-permute-done.1.refs_4_.refs_5_.rest_4_.rest_5_
  99.0 2.4 %collective-permute-start.9 = (bf16[16,256,128]{2,1,0:T(8,128)(2,1)}, bf16[16,256,128]{2,1,0:T(8,128)(2,1)}, u32[]{:S(2)}, u32[]{:S(2)}) collective-permute-start(bf16[16,256,128]{2,1,0:T(8,128)(2,1)} %get-tuple-element.83), channel_id=1, source_target_pairs={{0,24},{8,16},{16,8},{24,0},{1,25},{9,17},{17,9},{25,1},{2,26},{10... | collective-permute-start | bytes 3145736 | tf_op jit(solution)/shard_map/ppermute | solution.py:583
  101.3 0.1 broadcast_in_dim.31
  101.4 0.1 convert_element_type.32
  101.5 0.1 convert_element_type.33.frame_ref
  101.6 0.6 gather_fusion.2
  102.2 0.3 collective-permute-start.4
  102.5 0.0 collective-permute-start.5
  102.6 1.6 far_sums.5
  104.2 4.3 %far_sums.4 = f32[2,832]{1,0:T(2,128)S(1)} custom-call(bf16[2,20,208,128]{3,2,1,0:T(8,128)(2,1)S(1)} %copy-done.1, bf16[2,20,208,128]{3,2,1,0:T(8,128)(2,1)S(1)} %copy-done.1, bf16[2,20,208,128]{3,2,1,0:T(8,128)(2,1)} %collective-permute-done.refs_2_.refs_3_.rest_2_.rest_3_, bf16[2,20,208,128]{3,2,1,0:T(8,128)(2,1)} %collective-permute-done.refs_2_.refs_3_.rest_2_.rest_3_, ...), custom_call_target="tpu_custom_call" | custom-call | flops 6815744 | bytes 6815744 | tf_op jit(solution)/shard_map/far_sums/pallas_call | solution.py:345
  108.5 4.9 %psum.22 = f32[2,832]{1,0:T(2,128)S(1)} all-reduce(f32[2,832]{1,0:T(2,128)S(1)} %add.116), channel_id=1, replica_groups=mesh['tm'=4,'space'=2,'dp'=4] {'space'}, use_global_device_ids=true, to_apply=%region_1.0 | all-reduce | flops 1664 | bytes 13312 | tf_op jit(solution)/shard_map/psum | solution.py:413
  113.5 15.6 %temporal_weights.4.rest_4_ = bf16[16,13,64,128]{3,2,1,0:T(8,128)(2,1)} custom-call(s32[4]{0:T(128)S(1)} %get-tuple-element.61.slots_ref, s32[8,128]{1,0:T(8,128)S(1)} %bitcast.53, f32[2,896]{1,0:T(2,128)S(1)} %pad.8.factor_ref, f32[1,128]{1,0:T(1,128)S(1)} %convert_element_type.33.frame_ref, f32[20,1,128]{2,1,0:T(1,128)S(1)} %broadcast_in_dim.29.qg_ref, ...), custom_call_target="tpu_custom_call" | custom-call | flops 218103808 | bytes 8519680 | tf_op jit(solution)/shard_map/temporal_weights/pallas_call | solution.py:427
  129.0 1.2 collective-permute-start.6
  130.3 0.1 reduce_sum.9
  130.4 0.6 reduce_max.9
  131.7 0.6 gather_fusion.3
  132.4 1.6 conditional.1
  132.7 1.3 broadcast_in_dim.3
  133.9 0.1 add_xor_fusion
  134.0 0.1 pad_add_fusion.slots_ref
  134.1 1.0 copy-done.7
  135.1 4.7 %temporal_weights.5.rest_4_ = bf16[4,13,64,128]{3,2,1,0:T(8,128)(2,1)S(1)} custom-call(s32[4]{0:T(128)S(1)} %get-tuple-element.61.slots_ref, s32[8,128]{1,0:T(8,128)S(1)} %bitcast.55, f32[2,896]{1,0:T(2,128)S(1)} %pad.8.factor_ref, f32[1,128]{1,0:T(1,128)S(1)} %convert_element_type.33.frame_ref, f32[20,1,128]{2,1,0:T(1,128)S(1)} %broadcast_in_dim.29.qg_ref, ...), custom_call_target="tpu_custom_call" | custom-call | flops 54525952 | bytes 2129920 | tf_op jit(solution)/shard_map/temporal_weights/pallas_call | solution.py:427
  139.8 3.4 %collective-permute-done.9.rest_3_ = bf16[16,256,128]{2,1,0:T(8,128)(2,1)} collective-permute-done((bf16[16,256,128]{2,1,0:T(8,128)(2,1)}, bf16[16,256,128]{2,1,0:T(8,128)(2,1)}, u32[]{:S(2)}, u32[]{:S(2)}) %collective-permute-start.9) | collective-permute-done | bytes 1048608 | tf_op jit(solution)/shard_map/ppermute | solution.py:583
  143.2 6.3 %temporal_mix.2 = (f32[2,2,512]{2,1,0:T(2,128)S(1)}, f32[2,2,512]{2,1,0:T(2,128)S(1)}) custom-call(s32[8]{0:T(128)S(1)} %pad_add_fusion.slots_ref, s32[2,512]{1,0:T(2,128)S(1)} %get-tuple-element.58.rank_ref, f32[20,4,128]{2,1,0:T(4,128)S(1)} %bitcast.34, f32[20,1,128]{2,1,0:T(1,128)S(1)} %broadcast_in_dim.28.weight_ref, ...), custom_call_target="tpu_custom_call" | custom-call | flops 268435456 | bytes 6291456 | tf_op jit(solution)/shard_map/temporal_mix/pallas_call | solution.py:525
  149.6 0.5 collective-permute-done.5.rest_2_
  150.2 4.3 %collective-permute-done.6.rest_3_ = bf16[4,256,128]{2,1,0:T(8,128)(2,1)} collective-permute-done((bf16[4,256,128]{2,1,0:T(8,128)(2,1)}, bf16[4,256,128]{2,1,0:T(8,128)(2,1)}, u32[]{:S(2)}, u32[]{:S(2)}) %collective-permute-start.6) | collective-permute-done | bytes 262176 | tf_op jit(solution)/shard_map/ppermute | solution.py:583
  154.5 2.9 %temporal_mix.3 = (f32[2,2,512]{2,1,0:T(2,128)S(1)}, f32[2,2,512]{2,1,0:T(2,128)S(1)}) custom-call(s32[8]{0:T(128)S(1)} %pad_add_fusion.slots_ref, s32[2,512]{1,0:T(2,128)S(1)} %get-tuple-element.58.rank_ref, f32[20,4,128]{2,1,0:T(4,128)S(1)} %bitcast.35, f32[20,1,128]{2,1,0:T(1,128)S(1)} %broadcast_in_dim.28.weight_ref, ...), custom_call_target="tpu_custom_call" | custom-call | flops 67108864 | bytes 1572864 | tf_op jit(solution)/shard_map/temporal_mix/pallas_call | solution.py:525
  157.4 1.3 collective-permute-start.10
  158.7 0.8 collective-permute-done.10
  159.6 3.6 %collective-permute-start.11 = (f32[512]{0:T(512)S(1)}, f32[512]{0:T(512)S(1)}, u32[]{:S(2)}, u32[]{:S(2)}) collective-permute-start(f32[512]{0:T(512)S(1)} %bitcast.57), channel_id=1, source_target_pairs={{0,0},{16,4},{8,8},{24,12},{4,16},{20,20},{12,24},{28,28},{1,1},{1... | collective-permute-start | bytes 6152 | tf_op jit(solution)/shard_map/ppermute | solution.py:692
  163.2 1.3 collective-permute-start.12
  164.4 0.1 collective-permute-done.11
  164.5 2.6 %collective-permute-done.12 = f32[512]{0:T(512)S(1)} collective-permute-done((f32[512]{0:T(512)S(1)}, f32[512]{0:T(512)S(1)}, u32[]{:S(2)}, u32[]{:S(2)}) %collective-permute-start.12) | collective-permute-done | bytes 2080 | tf_op jit(solution)/shard_map/ppermute | solution.py:692
  167.1 0.6 add.122
  (46 shorter events, 0.2 us)
Async XLA Ops:
  0.0 131.7 %copy-start = (f32[4,20,128]{2,0,1:T(4,128)S(1)}, f32[4,20,128]{2,0,1:T(4,128)}, u32[]{:S(2)}) copy-start(f32[4,20,128]{2,0,1:T(4,128)} %param.13) | copy-start | bytes 122884
  0.0 6.4 %copy-start.11 = (s32[1024]{0:T(1024)S(1)}, s32[1024]{0:T(1024)}, u32[]{:S(2)}) copy-start(s32[1024]{0:T(1024)} %param.15) | copy-start | bytes 12292
  3.3 65.6 %collective-permute-start.2 = (bf16[2,4,208,128]{3,2,1,0:T(8,128)(2,1)S(1)}, bf16[2,4,208,128]{3,2,1,0:T(8,128)(2,1)S(1)}, u32[]{:S(2)}, u32[]{:S(2)}) collective-permute-start(bf16[2,4,208,128]{3,2,1,0:T(8,128)(2,1)S(1)} %get-tuple-element.59), channel_id=1, source_target_pairs={{0,24},{8,16},{16,8},{24,0},{1,25},{9,17},{17,9},{25,1},{2,26},{10... | collective-permute-start | bytes 1277960 | tf_op jit(solution)/shard_map/ppermute | solution.py:583
  12.1 18.9 %copy-start.12 = (f32[20,128]{1,0:T(8,128)S(1)}, f32[20,128]{1,0:T(8,128)}, u32[]{:S(2)}) copy-start(f32[20,128]{1,0:T(8,128)} %param.10) | copy-start | bytes 30724
  12.1 19.0 %copy-start.13 = (f32[20,128]{1,0:T(8,128)S(1)}, f32[20,128]{1,0:T(8,128)}, u32[]{:S(2)}) copy-start(f32[20,128]{1,0:T(8,128)} %param.11) | copy-start | bytes 30724
  12.1 69.0 %collective-permute-start.3 = (bf16[2,16,208,128]{3,2,1,0:T(8,128)(2,1)}, bf16[2,16,208,128]{3,2,1,0:T(8,128)(2,1)}, u32[]{:S(2)}, u32[]{:S(2)}) collective-permute-start(bf16[2,16,208,128]{3,2,1,0:T(8,128)(2,1)} %gather.28), channel_id=1, source_target_pairs={{0,24},{8,16},{16,8},{24,0},{1,25},{9,17},{17,9},{25,1},{2,26},{10... | collective-permute-start | bytes 5111816 | tf_op jit(solution)/shard_map/ppermute | solution.py:583
  24.5 73.7 %collective-permute-start = (bf16[2,20,208,128]{3,2,1,0:T(8,128)(2,1)}, bf16[2,20,208,128]{3,2,1,0:T(8,128)(2,1)}, u32[]{:S(2)}, u32[]{:S(2)}) collective-permute-start(bf16[2,20,208,128]{3,2,1,0:T(8,128)(2,1)} %get-tuple-element.65), channel_id=1, source_target_pairs={{0,8},{8,0},{16,24},{24,16},{1,9},{9,1},{17,25},{25,17},{2,10},{10... | collective-permute-start | bytes 6389768 | tf_op jit(solution)/shard_map/ppermute | solution.py:583
  25.9 73.1 %collective-permute-start.1 = (bf16[2,20,208,128]{3,2,1,0:T(8,128)(2,1)}, bf16[2,20,208,128]{3,2,1,0:T(8,128)(2,1)}, u32[]{:S(2)}, u32[]{:S(2)}) collective-permute-start(bf16[2,20,208,128]{3,2,1,0:T(8,128)(2,1)} %get-tuple-element.66), channel_id=1, source_target_pairs={{0,16},{8,24},{16,0},{24,8},{1,17},{9,25},{17,1},{25,9},{2,18},{10... | collective-permute-start | bytes 6389768 | tf_op jit(solution)/shard_map/ppermute | solution.py:583
  67.9 1.0 copy-start.8
  68.9 33.7 %copy-start.6 = (bf16[2,4,208,128]{3,2,1,0:T(8,128)(2,1)}, bf16[2,4,208,128]{3,2,1,0:T(8,128)(2,1)S(1)}, u32[]{:S(2)}) copy-start(bf16[2,4,208,128]{3,2,1,0:T(8,128)(2,1)S(1)} %collective-permute-done.2.refs_6_.refs_7_.rest_6_.rest_7_) | copy-start | bytes 1277956
  68.9 32.7 %copy-start.10 = (s32[4]{0:T(128)S(1)}, s32[4]{0:T(128)}, u32[]{:S(2)}) copy-start(s32[4]{0:T(128)} %param.14) | copy-start | bytes 52
  68.9 60.1 %collective-permute-start.8 = (bf16[16,256,128]{2,1,0:T(8,128)(2,1)}, bf16[16,256,128]{2,1,0:T(8,128)(2,1)}, u32[]{:S(2)}, u32[]{:S(2)}) collective-permute-start(bf16[16,256,128]{2,1,0:T(8,128)(2,1)} %get-tuple-element.81), channel_id=1, source_target_pairs={{0,16},{8,24},{16,0},{24,8},{1,17},{9,25},{17,1},{25,9},{2,18},{10... | collective-permute-start | bytes 3145736 | tf_op jit(solution)/shard_map/ppermute | solution.py:583
  69.1 33.5 %copy-start.1 = (bf16[2,20,208,128]{3,2,1,0:T(8,128)(2,1)S(1)}, bf16[2,20,208,128]{3,2,1,0:T(8,128)(2,1)}, u32[]{:S(2)}) copy-start(bf16[2,20,208,128]{3,2,1,0:T(8,128)(2,1)} %get-tuple-element.75.refs_0_.refs_1_.rest_0_.rest_1_) | copy-start | bytes 6389764
  80.8 59.0 %collective-permute-start.7 = (bf16[16,256,128]{2,1,0:T(8,128)(2,1)}, bf16[16,256,128]{2,1,0:T(8,128)(2,1)}, u32[]{:S(2)}, u32[]{:S(2)}) collective-permute-start(bf16[16,256,128]{2,1,0:T(8,128)(2,1)} %get-tuple-element.79), channel_id=1, source_target_pairs={{0,8},{8,0},{16,24},{24,16},{1,9},{9,1},{17,25},{25,17},{2,10},{10... | collective-permute-start | bytes 3145736 | tf_op jit(solution)/shard_map/ppermute | solution.py:583
  99.0 44.3 %collective-permute-start.9 = (bf16[16,256,128]{2,1,0:T(8,128)(2,1)}, bf16[16,256,128]{2,1,0:T(8,128)(2,1)}, u32[]{:S(2)}, u32[]{:S(2)}) collective-permute-start(bf16[16,256,128]{2,1,0:T(8,128)(2,1)} %get-tuple-element.83), channel_id=1, source_target_pairs={{0,24},{8,16},{16,8},{24,0},{1,25},{9,17},{17,9},{25,1},{2,26},{10... | collective-permute-start | bytes 3145736 | tf_op jit(solution)/shard_map/ppermute | solution.py:583
  102.2 47.4 %collective-permute-start.4 = (bf16[4,256,128]{2,1,0:T(8,128)(2,1)}, bf16[4,256,128]{2,1,0:T(8,128)(2,1)}, u32[]{:S(2)}, u32[]{:S(2)}) collective-permute-start(bf16[4,256,128]{2,1,0:T(8,128)(2,1)} %get-tuple-element.71), channel_id=1, source_target_pairs={{0,8},{8,0},{16,24},{24,16},{1,9},{9,1},{17,25},{25,17},{2,10},{10... | collective-permute-start | bytes 786440 | tf_op jit(solution)/shard_map/ppermute | solution.py:583
  102.5 47.6 %collective-permute-start.5 = (bf16[4,256,128]{2,1,0:T(8,128)(2,1)}, bf16[4,256,128]{2,1,0:T(8,128)(2,1)}, u32[]{:S(2)}, u32[]{:S(2)}) collective-permute-start(bf16[4,256,128]{2,1,0:T(8,128)(2,1)} %get-tuple-element.73), channel_id=1, source_target_pairs={{0,16},{8,24},{16,0},{24,8},{1,17},{9,25},{17,1},{25,9},{2,18},{10... | collective-permute-start | bytes 786440 | tf_op jit(solution)/shard_map/ppermute | solution.py:583
  113.5 18.2 %copy-start.14 = (f32[20,128]{1,0:T(8,128)S(1)}, f32[20,128]{1,0:T(8,128)}, u32[]{:S(2)}) copy-start(f32[20,128]{1,0:T(8,128)} %param.12) | copy-start | bytes 30724
  129.0 25.4 %collective-permute-start.6 = (bf16[4,256,128]{2,1,0:T(8,128)(2,1)}, bf16[4,256,128]{2,1,0:T(8,128)(2,1)}, u32[]{:S(2)}, u32[]{:S(2)}) collective-permute-start(bf16[4,256,128]{2,1,0:T(8,128)(2,1)} %get-tuple-element.76), channel_id=1, source_target_pairs={{0,24},{8,16},{16,8},{24,0},{1,25},{9,17},{17,9},{25,1},{2,26},{10... | collective-permute-start | bytes 786440 | tf_op jit(solution)/shard_map/ppermute | solution.py:583
  134.1 1.0 copy-start.7
  135.1 8.2 %copy-start.9 = (bf16[16,256,128]{2,1,0:T(8,128)(2,1)S(1)}, bf16[16,256,128]{2,1,0:T(8,128)(2,1)}, u32[]{:S(2)}) copy-start(bf16[16,256,128]{2,1,0:T(8,128)(2,1)} %copy-done.8) | copy-start | bytes 3145732
  157.4 2.1 %collective-permute-start.10 = (f32[2,2,512]{2,1,0:T(2,128)S(1)}, f32[2,2,512]{2,1,0:T(2,128)S(1)}, u32[]{:S(2)}, u32[]{:S(2)}) collective-permute-start(f32[2,2,512]{2,1,0:T(2,128)S(1)} %get-tuple-element.87), channel_id=1, source_target_pairs={{0,4},{4,0},{1,5},{5,1},{2,6},{6,2},{3,7},{7,3},{8,12},{12,8},{9,1... | collective-permute-start | bytes 24584 | tf_op jit(solution)/shard_map/ppermute | solution.py:683
  159.6 4.9 %collective-permute-start.11 = (f32[512]{0:T(512)S(1)}, f32[512]{0:T(512)S(1)}, u32[]{:S(2)}, u32[]{:S(2)}) collective-permute-start(f32[512]{0:T(512)S(1)} %bitcast.57), channel_id=1, source_target_pairs={{0,0},{16,4},{8,8},{24,12},{4,16},{20,20},{12,24},{28,28},{1,1},{1... | collective-permute-start | bytes 6152 | tf_op jit(solution)/shard_map/ppermute | solution.py:692
  163.2 4.0 %collective-permute-start.12 = (f32[512]{0:T(512)S(1)}, f32[512]{0:T(512)S(1)}, u32[]{:S(2)}, u32[]{:S(2)}) collective-permute-start(f32[512]{0:T(512)S(1)} %bitcast.56), channel_id=1, source_target_pairs={{8,0},{24,4},{0,8},{16,12},{12,16},{28,20},{4,24},{20,28},{9,1},{2... | collective-permute-start | bytes 6152 | tf_op jit(solution)/shard_map/ppermute | solution.py:692

commit v3 on v1

--- a/solution.py
+++ b/solution.py
@@ -393,47 +393,68 @@
     )(slots, counts, factors, frame, q_gain, k_gain, *[array for array, _, _ in far])
 
 
-def mix_kernel(slots_ref, count_ref, scale_ref, weight_ref, *rest, count, each, part, more):
+def mix_kernel(
+    slots_ref, count_ref, scale_ref, weight_ref, *rest, count, each, part, more, skips, size, whole
+):
     mixed, rest = rest[:count], rest[count:]
     weights, rest = rest[: -(count + 3 + more * count)], rest[-(count + 3 + more * count) :]
     before, rest = rest[: more * count], rest[more * count :]
     outs, (dot_ref, square_ref, rank_ref) = rest[:count], rest[count:]
-    head = pl.program_id(0)
     block = mixed[0].shape[1]
 
-    @pl.when(head == 0)
-    def _():
+    def begin():
         dot_ref[...] = jnp.zeros_like(dot_ref)
         square_ref[...] = jnp.zeros_like(square_ref)
         store_shares(count_ref, rank_ref)
 
-    subs = [(ref, j) for ref in weights for j in range(ref.shape[1])]
-    for sub, (p_ref, j) in enumerate(subs):
+    if whole:
+        begin()
+    else:
+        pl.when(pl.program_id(0) == 0)(begin)
+
+    subs = [(ref, skip, j) for ref, skip in zip(weights, skips) for j in range(ref.shape[1])]
+    for sub, (p_ref, skip, j) in enumerate(subs):
         at = sub * part
         dots = [dot_ref[slot, at : at + part] for slot in range(count)]
         squares = [square_ref[slot, at : at + part] for slot in range(count)]
-        for h in range(p_ref.shape[0]):
+        for h in range(size):
             o = jnp.concatenate([mixed[slot][h, at : at + part] for slot in range(count)], axis=0)
-            t = jnp.dot(p_ref[h, j], o, preferred_element_type=jnp.float32).astype(jnp.bfloat16)
+            t = jnp.dot(p_ref[skip + h, j], o, preferred_element_type=jnp.float32).astype(jnp.bfloat16)
             both = o.astype(jnp.float32) + t.astype(jnp.float32)
             for slot in range(count):
-                m = both[slot * part : (slot + 1) * part] * scale_ref[h, slot : slot + 1]
-                dots[slot] = dots[slot] + m * weight_ref[h]
+                m = both[slot * part : (slot + 1) * part] * scale_ref[skips[-1] + h, slot : slot + 1]
+                dots[slot] = dots[slot] + m * weight_ref[skips[-1] + h]
                 squares[slot] = squares[slot] + m * m
         for slot in range(count):
             dot_ref[slot, at : at + part] = dots[slot]
             square_ref[slot, at : at + part] = squares[slot]
 
-    @pl.when(head == pl.num_programs(0) - 1)
-    def _():
-        hit = picks(rank_ref, slots_ref[0], each, 0, block)
+    def end():
+        hit = jnp.where(picks(rank_ref, slots_ref[0], each, 0, block), 1.0, 0.0)
+        sums = [
+            lane_sums(ref[slots_ref[count + i]])
+            for i in range(count)
+            for ref in (dot_ref, square_ref)
+        ]
+        sums = jnp.concatenate(sums, axis=0)
+        high = sums.astype(jnp.bfloat16).astype(jnp.float32)
+        middle = (sums - high).astype(jnp.bfloat16).astype(jnp.float32)
+        terms = jnp.concatenate([high, middle, sums - high - middle], axis=0)
+        terms = jnp.dot(
+            terms.astype(jnp.bfloat16),
+            hit.astype(jnp.bfloat16),
+            preferred_element_type=jnp.float32,
+        )
+        number = 2 * count
+        placed = terms[:number] + terms[number : 2 * number] + terms[2 * number :]
         for i, out in enumerate(outs):
-            for which, ref in enumerate((dot_ref, square_ref)):
-                sums = jnp.sum(ref[slots_ref[count + i]], axis=1, keepdims=True)
-                sums = jnp.sum(jnp.where(hit, sums, 0.0), axis=0, keepdims=True)
-                if more:
-                    sums = before[i][which : which + 1] + sums
-                out[which : which + 1] = sums
+            mine = placed[2 * i : 2 * i + 2]
+            out[...] = before[i][...] + mine if more else mine
+
+    if whole:
+        end()
+    else:
+        pl.when(pl.program_id(0) == pl.num_programs(0) - 1)(end)
 
 
 def mix(slots, counts, weights, scales, weight, before, mixed, first, each, shares, part):
@@ -444,33 +465,59 @@
     width = counts.size // shares
     step = max(i for i in range(1, 6) if size % i == 0 and first % i == 0)
     skip = first // step
-    out = pl.BlockSpec((2, width), lambda h, s: (0, 0))
+    whole = len(before) > 0 and size == step
+    skips = tuple(first - at if whole else 0 for _, at in weights)
+    skips += (first if whole else 0,)
+    kernel = functools.partial(
+        mix_kernel,
+        count=count,
+        each=each,
+        part=part,
+        more=len(before) // count,
+        skips=skips,
+        size=step,
+        whole=whole,
+    )
+    scratch = [
+        pltpu.VMEM((count, block, HEAD), jnp.float32),
+        pltpu.VMEM((count, block, HEAD), jnp.float32),
+        pltpu.VMEM((shares, width), jnp.int32),
+    ]
+    operands = (slots, counts, scales, weight, *mixed, *[p for p, _ in weights], *before)
+    if whole:
+        held = pl.BlockSpec(memory_space=pltpu.VMEM)
+        layout = {
+            "in_specs": [pl.BlockSpec(memory_space=pltpu.SMEM)] + [held] * (len(operands) - 1),
+            "out_specs": [held] * count,
+            "scratch_shapes": scratch,
+        }
+    else:
+        out = pl.BlockSpec((2, width), lambda h, s: (0, 0))
+        layout = {
+            "grid_spec": pltpu.PrefetchScalarGridSpec(
+                num_scalar_prefetch=1,
+                grid=(size // step,),
+                in_specs=[
+                    pl.BlockSpec(counts.shape, lambda h, s: (0, 0)),
+                    pl.BlockSpec((step, count, HEAD), lambda h, s: (skip + h, 0, 0)),
+                    pl.BlockSpec((step, 1, HEAD), lambda h, s: (skip + h, 0, 0)),
+                ]
+                + [pl.BlockSpec((step, block, HEAD), lambda h, s: (h, 0, 0))] * count
+                + [
+                    pl.BlockSpec(
+                        (step, *p.shape[1:]),
+                        lambda h, s, skip=(first - at) // step: (skip + h, 0, 0, 0),
+                    )
+                    for p, at in weights
+                ]
+                + [out] * len(before),
+                out_specs=[out] * count,
+                scratch_shapes=scratch,
+            )
+        }
     return pl.pallas_call(
-        functools.partial(mix_kernel, count=count, each=each, part=part, more=len(before) // count),
-        grid_spec=pltpu.PrefetchScalarGridSpec(
-            num_scalar_prefetch=1,
-            grid=(size // step,),
-            in_specs=[
-                pl.BlockSpec(counts.shape, lambda h, s: (0, 0)),
-                pl.BlockSpec((step, count, HEAD), lambda h, s: (skip + h, 0, 0)),
-                pl.BlockSpec((step, 1, HEAD), lambda h, s: (skip + h, 0, 0)),
-            ]
-            + [pl.BlockSpec((step, block, HEAD), lambda h, s: (h, 0, 0))] * count
-            + [
-                pl.BlockSpec(
-                    (step, *p.shape[1:]),
-                    lambda h, s, skip=(first - at) // step: (skip + h, 0, 0, 0),
-                )
-                for p, at in weights
-            ]
-            + [out] * len(before),
-            out_specs=[out] * count,
-            scratch_shapes=[
-                pltpu.VMEM((count, block, HEAD), jnp.float32),
-                pltpu.VMEM((count, block, HEAD), jnp.float32),
-                pltpu.VMEM((shares, width), jnp.int32),
-            ],
-        ),
+        kernel,
+        **layout,
         out_shape=[jax.ShapeDtypeStruct((2, width), jnp.float32)] * count,
         compiler_params=pltpu.CompilerParams(vmem_limit_bytes=VMEM_LIMIT),
         cost_estimate=pl.CostEstimate(
@@ -479,7 +526,7 @@
             transcendentals=0,
         ),
         name="temporal_mix",
-    )(slots, counts, scales, weight, *mixed, *[p for p, _ in weights], *before)
+    )(*operands)
 
 
 def on_device(

time: 168 us -> 168 us (level)
  no operation moved by 1% of the time
where the time goes in v3:
time: 168 us; the launch traced here: 166 us
  Pallas kernels  103 us (61%)
  waiting for transfers between devices  29.9 us (18%)
  starting transfers between devices  16.6 us (10%)
  blocking collectives  8.86 us (5%)
  local copies, waits for them, and re-layouts  4.81 us (3%)
    pallas_call x2, Pallas kernels, spatial(): pl.pallas_call(functools.partial(spatial_kernel, count=count, each=each),...  48.3 us
    ppermute x10, waiting for transfers between devices, swap(): return lax.ppermute(value, 'tm', [(i, i ^ offset) for i in range(count)])  27.6 us
    pallas_call x3, Pallas kernels, gather(): pl.pallas_call(functools.partial(gather_kernel, offsets=tuple(offsets), e...  20.5 us
    pallas_call x2, Pallas kernels, temporal_weights(): pl.pallas_call(functools.partial(weights_kernel, each=each, first=first,...  18.8 us
    ppermute x10, starting transfers between devices, swap(): return lax.ppermute(value, 'tm', [(i, i ^ offset) for i in range(count)])  10.1 us
    pallas_call x2, Pallas kernels, mix(): pl.pallas_call(kernel, **layout, out_shape=[jax.ShapeDtypeStruct((2, widt...  9.34 us
    ppermute x4, starting transfers between devices, on_device(): sums = sums + lax.ppermute(total[r * shares + u], ('tm', 'space'), pairs)  6.5 us
    pallas_call x2, Pallas kernels, far_sums(): pl.pallas_call(far_sums_kernel, grid=(heads // step,), in_specs=[pl.Block...  5.92 us
  transfers between devices with their start and end apart: 14, of which 8 were waited for; matrix products, arithmetic and copies ran while one was open for 2% of the time, Pallas kernels for 59%

profile of v3, /device:TPU:1, one launch (start us, length us, event | category | flops | bytes accessed | tf_op | source)
XLA Modules:
  0.0 165.8 jit_solution(17420165752160438796)
XLA Ops:
  0.0 2.5 %gather.29 = bf16[2,4,208,128]{3,2,1,0:T(8,128)(2,1)S(1)} custom-call(s32[4]{0:T(128)S(1)} %iota_xor_fusion.slots_ref, s32[8,128]{1,0:T(8,128)} %bitcast.46, bf16[3,20,1024,128]{3,2,1,0:T(8,128)(2,1)} %bitcast.33, bf16[3,20,1024,128]{3,2,1,0:T(8,128)(2,1)} %bitcast.34), custom_call_target="tpu_custom_call" | custom-call | flops 2097152 | bytes 2523136 | tf_op jit(solution)/shard_map/gather/pallas_call | solution.py:147
  2.5 3.1 %collective-permute-start.2 = (bf16[2,4,208,128]{3,2,1,0:T(8,128)(2,1)S(1)}, bf16[2,4,208,128]{3,2,1,0:T(8,128)(2,1)S(1)}, u32[]{:S(2)}, u32[]{:S(2)}) collective-permute-start(bf16[2,4,208,128]{3,2,1,0:T(8,128)(2,1)S(1)} %gather.29), channel_id=1, source_target_pairs={{0,24},{8,16},{16,8},{24,0},{1,25},{9,17},{17,9},{25,1},{2,26},{10... | collective-permute-start | bytes 1277960 | tf_op jit(solution)/shard_map/ppermute | solution.py:546
  5.6 5.7 %gather.30 = bf16[2,16,208,128]{3,2,1,0:T(8,128)(2,1)} custom-call(s32[4]{0:T(128)S(1)} %iota_xor_fusion.slots_ref, s32[8,128]{1,0:T(8,128)S(1)} %bitcast.47, bf16[3,20,1024,128]{3,2,1,0:T(8,128)(2,1)} %bitcast.35, bf16[3,20,1024,128]{3,2,1,0:T(8,128)(2,1)} %bitcast.36), custom_call_target="tpu_custom_call" | custom-call | flops 8388608 | bytes 10092544 | tf_op jit(solution)/shard_map/gather/pallas_call | solution.py:147
  11.3 0.0 collective-permute-start.3
  11.3 12.3 %gather_sums.1 = (bf16[2,20,208,128]{3,2,1,0:T(8,128)(2,1)}, bf16[2,20,208,128]{3,2,1,0:T(8,128)(2,1)}, bf16[2,20,208,128]{3,2,1,0:T(8,128)(2,1)}, f32[2,1024]{1,0:T(2,128)S(1)}) custom-call(s32[4]{0:T(128)S(1)} %iota_xor_fusion.slots_ref, s32[8,128]{1,0:T(8,128)S(1)} %bitcast.48, bf16[3,20,1024,128]{3,2,1,0:T(8,128)(2,1)} %bitcast.37, ...), custom_call_target="tpu_custom_call" | custom-call | flops 10485760 | bytes 16875520 | tf_op jit(solution)/shard_map/gather_sums/pallas_call | solution.py:147
  23.6 1.4 collective-permute-start
  25.0 1.2 collective-permute-start.1
  26.2 4.0 %psum.21 = f32[2,1024]{1,0:T(2,128)S(1)} all-reduce(f32[2,1024]{1,0:T(2,128)S(1)} %get-tuple-element.62), channel_id=1, replica_groups=mesh['tm'=4,'space'=2,'dp'=4] {'space'}, use_global_device_ids=true, to_apply=%region_0.0 | all-reduce | flops 2048 | bytes 16384 | tf_op jit(solution)/shard_map/psum | solution.py:561
  30.2 36.6 %spatial_attention.3 = (bf16[16,256,128]{2,1,0:T(8,128)(2,1)S(1)}, bf16[16,256,128]{2,1,0:T(8,128)(2,1)}, bf16[16,256,128]{2,1,0:T(8,128)(2,1)}, bf16[16,256,128]{2,1,0:T(8,128)(2,1)}) custom-call(s32[4]{0:T(128)S(1)} %iota_xor_fusion.slots_ref, s32[8,128]{1,0:T(8,128)S(1)} %bitcast.49, bf16[3,20,1024,128]{3,2,1,0:T(8,128)(2,1)} %bitcast.39, ...), custom_call_target="tpu_custom_call" | custom-call | flops 17179869184 | bytes 16777216 | tf_op jit(solution)/shard_map/spatial_attention/pallas_call | solution.py:217
  66.9 1.0 copy-done.8
  67.9 0.2 collective-permute-start.8
  68.1 11.6 %spatial_attention.2 = (bf16[4,256,128]{2,1,0:T(8,128)(2,1)S(1)}, bf16[4,256,128]{2,1,0:T(8,128)(2,1)}, bf16[4,256,128]{2,1,0:T(8,128)(2,1)}, bf16[4,256,128]{2,1,0:T(8,128)(2,1)}) custom-call(s32[4]{0:T(128)S(1)} %iota_xor_fusion.slots_ref, s32[8,128]{1,0:T(8,128)S(1)} %bitcast.50, bf16[3,20,1024,128]{3,2,1,0:T(8,128)(2,1)} %bitcast.42, ...), custom_call_target="tpu_custom_call" | custom-call | flops 4294967296 | bytes 4194304 | tf_op jit(solution)/shard_map/spatial_attention/pallas_call | solution.py:217
  79.8 0.3 collective-permute-start.7
  80.0 17.4 %collective-permute-done.refs_2_.refs_3_.rest_2_.rest_3_ = bf16[2,20,208,128]{3,2,1,0:T(8,128)(2,1)} collective-permute-done((bf16[2,20,208,128]{3,2,1,0:T(8,128)(2,1)}, bf16[2,20,208,128]{3,2,1,0:T(8,128)(2,1)}, u32[]{:S(2)}, u32[]{:S(2)}) %collective-permute-start) | collective-permute-done | bytes 2129952 | tf_op jit(solution)/shard_map/ppermute | solution.py:546
  97.4 0.8 collective-permute-done.1.refs_4_.refs_5_.rest_4_.rest_5_
  98.1 2.4 %collective-permute-start.9 = (bf16[16,256,128]{2,1,0:T(8,128)(2,1)}, bf16[16,256,128]{2,1,0:T(8,128)(2,1)}, u32[]{:S(2)}, u32[]{:S(2)}) collective-permute-start(bf16[16,256,128]{2,1,0:T(8,128)(2,1)} %get-tuple-element.83), channel_id=1, source_target_pairs={{0,24},{8,16},{16,8},{24,0},{1,25},{9,17},{17,9},{25,1},{2,26},{10... | collective-permute-start | bytes 3145736 | tf_op jit(solution)/shard_map/ppermute | solution.py:546
  100.5 0.1 broadcast_in_dim.29
  100.6 0.1 convert_element_type.28.frame_ref
  100.7 0.6 gather_fusion.2
  101.3 0.3 collective-permute-start.4
  101.6 0.1 collective-permute-start.5
  101.7 1.6 far_sums.5
  103.3 4.3 %far_sums.4 = f32[2,832]{1,0:T(2,128)S(1)} custom-call(bf16[2,20,208,128]{3,2,1,0:T(8,128)(2,1)S(1)} %copy-done.1, bf16[2,20,208,128]{3,2,1,0:T(8,128)(2,1)S(1)} %copy-done.1, bf16[2,20,208,128]{3,2,1,0:T(8,128)(2,1)} %collective-permute-done.refs_2_.refs_3_.rest_2_.rest_3_, bf16[2,20,208,128]{3,2,1,0:T(8,128)(2,1)} %collective-permute-done.refs_2_.refs_3_.rest_2_.rest_3_, ...), custom_call_target="tpu_custom_call" | custom-call | flops 6815744 | bytes 6815744 | tf_op jit(solution)/shard_map/far_sums/pallas_call | solution.py:280
  107.6 4.9 %psum.22 = f32[2,832]{1,0:T(2,128)S(1)} all-reduce(f32[2,832]{1,0:T(2,128)S(1)} %add.121), channel_id=1, replica_groups=mesh['tm'=4,'space'=2,'dp'=4] {'space'}, use_global_device_ids=true, to_apply=%region_1.0 | all-reduce | flops 1664 | bytes 13312 | tf_op jit(solution)/shard_map/psum | solution.py:344
  112.6 14.4 %temporal_weights.4.rest_4_ = bf16[16,13,64,64]{3,2,1,0:T(8,128)(2,1)} custom-call(s32[4]{0:T(128)S(1)} %iota_xor_fusion.slots_ref, s32[8,128]{1,0:T(8,128)S(1)} %bitcast.51, f32[2,896]{1,0:T(2,128)S(1)} %pad.8.factor_ref, f32[1,64]{1,0:T(1,128)S(1)} %convert_element_type.28.frame_ref, f32[20,1,128]{2,1,0:T(1,128)S(1)} %broadcast_in_dim.27.qg_ref, ...), custom_call_target="tpu_custom_call" | custom-call | flops 218103808 | bytes 8519680 | tf_op jit(solution)/shard_map/temporal_weights/pallas_call | solution.py:358
  127.0 1.2 collective-permute-start.6
  128.2 0.1 reduce_sum.9
  128.4 0.7 reduce_max.9
  129.7 0.6 gather_fusion.3
  130.4 1.6 conditional.1
  130.7 1.3 broadcast_in_dim.4
  132.0 0.1 add_xor_fusion
  132.0 0.1 pad_add_fusion.slots_ref
  132.1 1.0 copy-done.7
  133.1 4.4 %temporal_weights.5.rest_4_ = bf16[4,13,64,64]{3,2,1,0:T(8,128)(2,1)S(1)} custom-call(s32[4]{0:T(128)S(1)} %iota_xor_fusion.slots_ref, s32[8,128]{1,0:T(8,128)S(1)} %bitcast.53, f32[2,896]{1,0:T(2,128)S(1)} %pad.8.factor_ref, f32[1,64]{1,0:T(1,128)S(1)} %convert_element_type.28.frame_ref, f32[20,1,128]{2,1,0:T(1,128)S(1)} %broadcast_in_dim.27.qg_ref, ...), custom_call_target="tpu_custom_call" | custom-call | flops 54525952 | bytes 2129920 | tf_op jit(solution)/shard_map/temporal_weights/pallas_call | solution.py:358
  137.5 4.9 %collective-permute-done.9.rest_3_ = bf16[16,256,128]{2,1,0:T(8,128)(2,1)} collective-permute-done((bf16[16,256,128]{2,1,0:T(8,128)(2,1)}, bf16[16,256,128]{2,1,0:T(8,128)(2,1)}, u32[]{:S(2)}, u32[]{:S(2)}) %collective-permute-start.9) | collective-permute-done | bytes 1048608 | tf_op jit(solution)/shard_map/ppermute | solution.py:546
  142.4 6.7 %temporal_mix.2 = (f32[2,512]{1,0:T(2,128)S(1)}, f32[2,512]{1,0:T(2,128)S(1)}, f32[2,512]{1,0:T(2,128)S(1)}, f32[2,512]{1,0:T(2,128)S(1)}) custom-call(s32[8]{0:T(128)S(1)} %pad_add_fusion.slots_ref, s32[8,128]{1,0:T(8,128)S(1)} %bitcast.54, f32[20,4,128]{2,1,0:T(4,128)S(1)} %bitcast.31, f32[20,1,128]{2,1,0:T(1,128)S(1)} %broadcast_in_dim.26.weight_ref, ...), custom_call_target="tpu_custom_call" | custom-call | flops 268435456 | bytes 6291456 | tf_op jit(solution)/shard_map/temporal_mix/pallas_call | solution.py:518
  149.1 0.2 collective-permute-done.5.rest_2_
  149.3 4.3 %collective-permute-done.6.rest_3_ = bf16[4,256,128]{2,1,0:T(8,128)(2,1)} collective-permute-done((bf16[4,256,128]{2,1,0:T(8,128)(2,1)}, bf16[4,256,128]{2,1,0:T(8,128)(2,1)}, u32[]{:S(2)}, u32[]{:S(2)}) %collective-permute-start.6) | collective-permute-done | bytes 262176 | tf_op jit(solution)/shard_map/ppermute | solution.py:546
  153.7 2.7 %temporal_mix.3 = (f32[2,512]{1,0:T(2,128)S(1)}, f32[2,512]{1,0:T(2,128)S(1)}, f32[2,512]{1,0:T(2,128)S(1)}, f32[2,512]{1,0:T(2,128)S(1)}) custom-call(s32[8]{0:T(128)S(1)} %pad_add_fusion.slots_ref, s32[8,128]{1,0:T(8,128)S(1)} %bitcast.55, f32[20,4,128]{2,1,0:T(4,128)S(1)} %bitcast.32, f32[20,1,128]{2,1,0:T(1,128)S(1)} %broadcast_in_dim.26.weight_ref, ...), custom_call_target="tpu_custom_call" | custom-call | flops 67108864 | bytes 1572864 | tf_op jit(solution)/shard_map/temporal_mix/pallas_call | solution.py:518
  156.4 4.5 %collective-permute-start.10 = (f32[2,512]{1,0:T(2,128)S(1)}, f32[2,512]{1,0:T(2,128)S(1)}, u32[]{:S(2)}, u32[]{:S(2)}) collective-permute-start(f32[2,512]{1,0:T(2,128)S(1)} %get-tuple-element.88), channel_id=1, source_target_pairs={{0,0},{16,4},{8,8},{24,12},{4,16},{20,20},{12,24},{28,28},{1,1},{1... | collective-permute-start | bytes 12296 | tf_op jit(solution)/shard_map/ppermute | solution.py:648
  160.8 0.0 collective-permute-start.11
  160.8 1.0 collective-permute-start.12
  161.8 1.0 collective-permute-start.13
  162.9 0.4 collective-permute-done.11
  163.3 1.5 collective-permute-done.12
  164.8 0.4 collective-permute-done.13
  165.2 0.6 fusion.10
  (46 shorter events, 0.2 us)
Async XLA Ops:
  0.0 129.7 %copy-start = (f32[4,20,128]{2,0,1:T(4,128)S(1)}, f32[4,20,128]{2,0,1:T(4,128)}, u32[]{:S(2)}) copy-start(f32[4,20,128]{2,0,1:T(4,128)} %param.13) | copy-start | bytes 122884
  0.0 5.6 %copy-start.11 = (s32[1024]{0:T(1024)S(1)}, s32[1024]{0:T(1024)}, u32[]{:S(2)}) copy-start(s32[1024]{0:T(1024)} %param.15) | copy-start | bytes 12292
  2.5 65.3 %collective-permute-start.2 = (bf16[2,4,208,128]{3,2,1,0:T(8,128)(2,1)S(1)}, bf16[2,4,208,128]{3,2,1,0:T(8,128)(2,1)S(1)}, u32[]{:S(2)}, u32[]{:S(2)}) collective-permute-start(bf16[2,4,208,128]{3,2,1,0:T(8,128)(2,1)S(1)} %gather.29), channel_id=1, source_target_pairs={{0,24},{8,16},{16,8},{24,0},{1,25},{9,17},{17,9},{25,1},{2,26},{10... | collective-permute-start | bytes 1277960 | tf_op jit(solution)/shard_map/ppermute | solution.py:546
  11.3 14.9 %copy-start.12 = (f32[20,128]{1,0:T(8,128)S(1)}, f32[20,128]{1,0:T(8,128)}, u32[]{:S(2)}) copy-start(f32[20,128]{1,0:T(8,128)} %param.10) | copy-start | bytes 30724
  11.3 14.9 %copy-start.13 = (f32[20,128]{1,0:T(8,128)S(1)}, f32[20,128]{1,0:T(8,128)}, u32[]{:S(2)}) copy-start(f32[20,128]{1,0:T(8,128)} %param.11) | copy-start | bytes 30724
  11.3 68.7 %collective-permute-start.3 = (bf16[2,16,208,128]{3,2,1,0:T(8,128)(2,1)}, bf16[2,16,208,128]{3,2,1,0:T(8,128)(2,1)}, u32[]{:S(2)}, u32[]{:S(2)}) collective-permute-start(bf16[2,16,208,128]{3,2,1,0:T(8,128)(2,1)} %gather.30), channel_id=1, source_target_pairs={{0,24},{8,16},{16,8},{24,0},{1,25},{9,17},{17,9},{25,1},{2,26},{10... | collective-permute-start | bytes 5111816 | tf_op jit(solution)/shard_map/ppermute | solution.py:546
  23.6 73.8 %collective-permute-start = (bf16[2,20,208,128]{3,2,1,0:T(8,128)(2,1)}, bf16[2,20,208,128]{3,2,1,0:T(8,128)(2,1)}, u32[]{:S(2)}, u32[]{:S(2)}) collective-permute-start(bf16[2,20,208,128]{3,2,1,0:T(8,128)(2,1)} %get-tuple-element.65), channel_id=1, source_target_pairs={{0,8},{8,0},{16,24},{24,16},{1,9},{9,1},{17,25},{25,17},{2,10},{10... | collective-permute-start | bytes 6389768 | tf_op jit(solution)/shard_map/ppermute | solution.py:546
  25.0 73.2 %collective-permute-start.1 = (bf16[2,20,208,128]{3,2,1,0:T(8,128)(2,1)}, bf16[2,20,208,128]{3,2,1,0:T(8,128)(2,1)}, u32[]{:S(2)}, u32[]{:S(2)}) collective-permute-start(bf16[2,20,208,128]{3,2,1,0:T(8,128)(2,1)} %get-tuple-element.66), channel_id=1, source_target_pairs={{0,16},{8,24},{16,0},{24,8},{1,17},{9,25},{17,1},{25,9},{2,18},{10... | collective-permute-start | bytes 6389768 | tf_op jit(solution)/shard_map/ppermute | solution.py:546
  66.9 1.0 copy-start.8
  67.9 33.8 %copy-start.6 = (bf16[2,4,208,128]{3,2,1,0:T(8,128)(2,1)}, bf16[2,4,208,128]{3,2,1,0:T(8,128)(2,1)S(1)}, u32[]{:S(2)}) copy-start(bf16[2,4,208,128]{3,2,1,0:T(8,128)(2,1)S(1)} %collective-permute-done.2.refs_6_.refs_7_.rest_6_.rest_7_) | copy-start | bytes 1277956
  67.9 32.8 %copy-start.10 = (s32[4]{0:T(128)S(1)}, s32[4]{0:T(128)}, u32[]{:S(2)}) copy-start(s32[4]{0:T(128)} %param.14) | copy-start | bytes 52
  67.9 59.1 %collective-permute-start.8 = (bf16[16,256,128]{2,1,0:T(8,128)(2,1)}, bf16[16,256,128]{2,1,0:T(8,128)(2,1)}, u32[]{:S(2)}, u32[]{:S(2)}) collective-permute-start(bf16[16,256,128]{2,1,0:T(8,128)(2,1)} %get-tuple-element.81), channel_id=1, source_target_pairs={{0,16},{8,24},{16,0},{24,8},{1,17},{9,25},{17,1},{25,9},{2,18},{10... | collective-permute-start | bytes 3145736 | tf_op jit(solution)/shard_map/ppermute | solution.py:546
  68.1 33.6 %copy-start.1 = (bf16[2,20,208,128]{3,2,1,0:T(8,128)(2,1)S(1)}, bf16[2,20,208,128]{3,2,1,0:T(8,128)(2,1)}, u32[]{:S(2)}) copy-start(bf16[2,20,208,128]{3,2,1,0:T(8,128)(2,1)} %get-tuple-element.75.refs_0_.refs_1_.rest_0_.rest_1_) | copy-start | bytes 6389764
  79.8 57.7 %collective-permute-start.7 = (bf16[16,256,128]{2,1,0:T(8,128)(2,1)}, bf16[16,256,128]{2,1,0:T(8,128)(2,1)}, u32[]{:S(2)}, u32[]{:S(2)}) collective-permute-start(bf16[16,256,128]{2,1,0:T(8,128)(2,1)} %get-tuple-element.79), channel_id=1, source_target_pairs={{0,8},{8,0},{16,24},{24,16},{1,9},{9,1},{17,25},{25,17},{2,10},{10... | collective-permute-start | bytes 3145736 | tf_op jit(solution)/shard_map/ppermute | solution.py:546
  98.1 44.3 %collective-permute-start.9 = (bf16[16,256,128]{2,1,0:T(8,128)(2,1)}, bf16[16,256,128]{2,1,0:T(8,128)(2,1)}, u32[]{:S(2)}, u32[]{:S(2)}) collective-permute-start(bf16[16,256,128]{2,1,0:T(8,128)(2,1)} %get-tuple-element.83), channel_id=1, source_target_pairs={{0,24},{8,16},{16,8},{24,0},{1,25},{9,17},{17,9},{25,1},{2,26},{10... | collective-permute-start | bytes 3145736 | tf_op jit(solution)/shard_map/ppermute | solution.py:546
  101.3 47.8 %collective-permute-start.4 = (bf16[4,256,128]{2,1,0:T(8,128)(2,1)}, bf16[4,256,128]{2,1,0:T(8,128)(2,1)}, u32[]{:S(2)}, u32[]{:S(2)}) collective-permute-start(bf16[4,256,128]{2,1,0:T(8,128)(2,1)} %get-tuple-element.71), channel_id=1, source_target_pairs={{0,8},{8,0},{16,24},{24,16},{1,9},{9,1},{17,25},{25,17},{2,10},{10... | collective-permute-start | bytes 786440 | tf_op jit(solution)/shard_map/ppermute | solution.py:546
  101.6 47.7 %collective-permute-start.5 = (bf16[4,256,128]{2,1,0:T(8,128)(2,1)}, bf16[4,256,128]{2,1,0:T(8,128)(2,1)}, u32[]{:S(2)}, u32[]{:S(2)}) collective-permute-start(bf16[4,256,128]{2,1,0:T(8,128)(2,1)} %get-tuple-element.73), channel_id=1, source_target_pairs={{0,16},{8,24},{16,0},{24,8},{1,17},{9,25},{17,1},{25,9},{2,18},{10... | collective-permute-start | bytes 786440 | tf_op jit(solution)/shard_map/ppermute | solution.py:546
  112.6 17.1 %copy-start.14 = (f32[20,128]{1,0:T(8,128)S(1)}, f32[20,128]{1,0:T(8,128)}, u32[]{:S(2)}) copy-start(f32[20,128]{1,0:T(8,128)} %param.12) | copy-start | bytes 30724
  127.0 26.7 %collective-permute-start.6 = (bf16[4,256,128]{2,1,0:T(8,128)(2,1)}, bf16[4,256,128]{2,1,0:T(8,128)(2,1)}, u32[]{:S(2)}, u32[]{:S(2)}) collective-permute-start(bf16[4,256,128]{2,1,0:T(8,128)(2,1)} %get-tuple-element.76), channel_id=1, source_target_pairs={{0,24},{8,16},{16,8},{24,0},{1,25},{9,17},{17,9},{25,1},{2,26},{10... | collective-permute-start | bytes 786440 | tf_op jit(solution)/shard_map/ppermute | solution.py:546
  132.1 1.0 copy-start.7
  133.1 9.3 %copy-start.9 = (bf16[16,256,128]{2,1,0:T(8,128)(2,1)S(1)}, bf16[16,256,128]{2,1,0:T(8,128)(2,1)}, u32[]{:S(2)}) copy-start(bf16[16,256,128]{2,1,0:T(8,128)(2,1)} %copy-done.8) | copy-start | bytes 3145732
  156.4 6.5 %collective-permute-start.10 = (f32[2,512]{1,0:T(2,128)S(1)}, f32[2,512]{1,0:T(2,128)S(1)}, u32[]{:S(2)}, u32[]{:S(2)}) collective-permute-start(f32[2,512]{1,0:T(2,128)S(1)} %get-tuple-element.88), channel_id=1, source_target_pairs={{0,0},{16,4},{8,8},{24,12},{4,16},{20,20},{12,24},{28,28},{1,1},{1... | collective-permute-start | bytes 12296 | tf_op jit(solution)/shard_map/ppermute | solution.py:648
  160.8 2.5 %collective-permute-start.11 = (f32[2,512]{1,0:T(2,128)S(1)}, f32[2,512]{1,0:T(2,128)S(1)}, u32[]{:S(2)}, u32[]{:S(2)}) collective-permute-start(f32[2,512]{1,0:T(2,128)S(1)} %get-tuple-element.89), channel_id=1, source_target_pairs={{4,0},{20,4},{12,8},{28,12},{0,16},{16,20},{8,24},{24,28},{5,1},{2... | collective-permute-start | bytes 12296 | tf_op jit(solution)/shard_map/ppermute | solution.py:648
  160.8 4.0 %collective-permute-start.12 = (f32[2,512]{1,0:T(2,128)S(1)}, f32[2,512]{1,0:T(2,128)S(1)}, u32[]{:S(2)}, u32[]{:S(2)}) collective-permute-start(f32[2,512]{1,0:T(2,128)S(1)} %get-tuple-element.90), channel_id=1, source_target_pairs={{8,0},{24,4},{0,8},{16,12},{12,16},{28,20},{4,24},{20,28},{9,1},{2... | collective-permute-start | bytes 12296 | tf_op jit(solution)/shard_map/ppermute | solution.py:648
  161.8 3.4 %collective-permute-start.13 = (f32[2,512]{1,0:T(2,128)S(1)}, f32[2,512]{1,0:T(2,128)S(1)}, u32[]{:S(2)}, u32[]{:S(2)}) collective-permute-start(f32[2,512]{1,0:T(2,128)S(1)} %get-tuple-element.91), channel_id=1, source_target_pairs={{12,0},{28,4},{4,8},{20,12},{8,16},{24,20},{0,24},{16,28},{13,1},{... | collective-permute-start | bytes 12296 | tf_op jit(solution)/shard_map/ppermute | solution.py:648
